TPU v7x, 512 devices: a whole 4x8x8 slice. The times are simulated.
512 devices in a mesh: blk: 64 (over y_hi, x, z), group: 8 (over y_lo, core).
Axes of the slice: x: 4, y: 8 (y_hi: 2, y_lo: 4; y = y_hi * 4 + y_lo), z: 8, core: 2. Of those that a mesh axis runs over, the one named last changes fastest.
Arguments:
- images: bfloat16 [65536, 1152], P(('blk', 'group')), may hold values from -0.1875 to 0.1875
- captions: bfloat16 [65536, 1152], P(('blk', 'group')), may hold values from -0.1875 to 0.1875
- labels: int32 [65536], P(('blk', 'group')), may hold values from 0 to 1023
- logit_scale: float32 [1], replicated, may hold values from 4 to 12
- logit_bias: float32 [1], replicated, may hold values from -6 to -3
Outputs:
- loss_rows: float32 [65536], P(('blk', 'group'))
- image_grad: float32 [65536, 1152], P(('blk', 'group'))
- text_grad: float32 [65536, 1152], P(('blk', 'group'))
Inputs may be any that keep to these rules, and one draw needn't show every extreme that they name: `labels`: the positive caption of an image in block b is caption row b * 1024 + label.
All inputs are finite; a program needn't handle non-finite values.
Results may differ from a plain program's by a relative error of at most 0.015.
Values may be sent and summed in bfloat16 or wider, within the bound.
A program may use at most 64 MiB of HBM per device.

v0:
```python
import jax
import jax.numpy as jnp
from jax import lax
from jax.sharding import PartitionSpec as P

EPSILON = 1e-06


def from_behind(value, axis, steps):
    count = lax.axis_size(axis)
    pairs = [(source, (source + steps) % count) for source in range(count)]
    return lax.ppermute(value, axis, pairs)


def unit_rows(values):
    wide = values.astype(jnp.float32)
    length = jnp.sqrt(jnp.sum(wide * wide, axis=-1, keepdims=True) + EPSILON)
    return (wide / length, length)


def pair_tile(image_unit, text_block, labels, diagonal, scale_value, bias_value):
    raw = lax.dot_general(
        image_unit, text_block, (((1,), (1,)), ((), ())), preferred_element_type=jnp.float32
    )
    logits = scale_value * raw + bias_value
    columns = lax.broadcasted_iota(jnp.int32, logits.shape, 1)
    positive = jnp.logical_and(diagonal, columns == labels[:, None])
    signed = jnp.where(positive, logits, -logits)
    row_loss = -jnp.sum(jax.nn.log_sigmoid(signed), axis=1)
    slope = jnp.where(positive, -1.0, 1.0) * jax.nn.sigmoid(-signed)
    weights = (scale_value * slope).astype(jnp.bfloat16)
    image_part = jnp.dot(weights, text_block, preferred_element_type=jnp.float32)
    text_part = lax.dot_general(
        weights, image_unit, (((0,), (0,)), ((), ())), preferred_element_type=jnp.float32
    )
    return (row_loss, image_part, text_part.astype(jnp.bfloat16))


def through_norm(sums, unit_float, length):
    return (sums - unit_float * jnp.sum(unit_float * sums, axis=-1, keepdims=True)) / length


def per_device(images, captions, labels, logit_scale, logit_bias):
    scale_value = logit_scale[0]
    bias_value = logit_bias[0]
    image_float, image_length = unit_rows(images)
    image_unit = image_float.astype(jnp.bfloat16)
    text_float, text_length = unit_rows(captions)
    text_unit = text_float.astype(jnp.bfloat16)
    own_block = lax.all_gather(text_unit, "group", axis=0, tiled=True)
    lower_block = from_behind(own_block, "blk", 1)
    upper_block = from_behind(own_block, "blk", -1)
    lower_loss, lower_image, lower_bits = pair_tile(
        image_unit, lower_block, labels, False, scale_value, bias_value
    )
    own_loss, own_image, own_bits = pair_tile(
        image_unit, own_block, labels, True, scale_value, bias_value
    )
    upper_loss, upper_image, upper_bits = pair_tile(
        image_unit, upper_block, labels, False, scale_value, bias_value
    )
    from_above = from_behind(lower_bits, "blk", -1)
    from_below = from_behind(upper_bits, "blk", 1)
    partial_value = from_above.astype(jnp.float32) + lax.optimization_barrier(own_bits).astype(
        jnp.float32
    )
    partial_value = partial_value + from_below.astype(jnp.float32)
    text_sums = lax.psum_scatter(
        partial_value.astype(jnp.bfloat16), "group", scatter_dimension=0, tiled=True
    ).astype(jnp.float32)
    loss_rows = lower_loss + own_loss + upper_loss
    image_sums = lower_image + own_image + upper_image
    image_grad = through_norm(image_sums, image_float, image_length)
    text_grad = through_norm(text_sums, text_float, text_length)
    return (loss_rows, image_grad, text_grad)


def solution(mesh):
    in_specs = (P(("blk", "group"), None), P(("blk", "group"), None), P(("blk", "group")), P(), P())
    out_specs = (P(("blk", "group")), P(("blk", "group"), None), P(("blk", "group"), None))
    return jax.shard_map(
        per_device, mesh=mesh, in_specs=in_specs, out_specs=out_specs, check_vma=False
    )
```

profile of v0, /device:TPU:1, one launch (start us, length us, event | category | flops | bytes accessed | tf_op | source)
XLA Modules:
  0.0 328.6 jit_solution(15747951220828750233)
XLA Ops:
  7.2 1.1 fusion.5
  8.3 1.8 fusion.12
  10.2 46.8 %all-gather.2.cloned.1.call-done = bf16[1024,1152]{1,0:T(8,128)(2,1)} async-done(((bf16[128,1152]{1,0:T(8,128)(2,1)}), bf16[1024,1152]{1,0:T(8,128)(2,1)}) %all-gather.2.cloned.1.call-update) | async-done | bytes 2359312 | tf_op jit(solution)/shard_map/all_gather | solution.py:50
  57.0 11.0 %collective-permute-start.1 = (bf16[1024,1152]{1,0:T(8,128)(2,1)}, bf16[1024,1152]{1,0:T(8,128)(2,1)S(1)}, u32[]{:S(2)}, u32[]{:S(2)}) collective-permute-start(bf16[1024,1152]{1,0:T(8,128)(2,1)} %all-gather.2.cloned.1.call-done), channel_id=1, source_target_pairs={{0,504},{8,0},{16,8},{24,16},{32,24},{40,32},{48,40},{56,48},{64,5... | collective-permute-start | bytes 7077896 | tf_op jit(solution)/shard_map/ppermute | solution.py:12
  68.0 1.9 collective-permute-start
  71.3 1.1 fusion.4
  72.4 96.7 %collective-permute-done.1 = bf16[1024,1152]{1,0:T(8,128)(2,1)S(1)} collective-permute-done((bf16[1024,1152]{1,0:T(8,128)(2,1)}, bf16[1024,1152]{1,0:T(8,128)(2,1)S(1)}, u32[]{:S(2)}, u32[]{:S(2)}) %collective-permute-start.1) | collective-permute-done | bytes 2359328 | tf_op jit(solution)/shard_map/ppermute | solution.py:12
  169.1 2.4 fusion.10
  171.5 0.8 convolution_convert_fusion
  172.3 1.9 collective-permute-start.3
  174.3 43.6 %collective-permute-done = bf16[1024,1152]{1,0:T(8,128)(2,1)S(1)} collective-permute-done((bf16[1024,1152]{1,0:T(8,128)(2,1)}, bf16[1024,1152]{1,0:T(8,128)(2,1)S(1)}, u32[]{:S(2)}, u32[]{:S(2)}) %collective-permute-start) | collective-permute-done | bytes 2359328 | tf_op jit(solution)/shard_map/ppermute | solution.py:12
  217.9 1.1 fusion.8
  219.3 0.8 convolution_convert_fusion.2
  220.2 2.1 collective-permute-start.2
  222.2 1.2 fusion.9
  223.4 0.9 convolution_convert_fusion.1
  224.4 57.6 %collective-permute-done.3 = bf16[1024,1152]{1,0:T(8,128)(2,1)S(1)} collective-permute-done((bf16[1024,1152]{1,0:T(8,128)(2,1)S(1)}, bf16[1024,1152]{1,0:T(8,128)(2,1)S(1)}, u32[]{:S(2)}, u32[]{:S(2)}) %collective-permute-start.3) | collective-permute-done | bytes 2359328 | tf_op jit(solution)/shard_map/ppermute | solution.py:12
  282.0 2.3 add_convert_fusion
  284.3 1.8 fusion.14
  287.9 0.7 multiply_reduce_fusion
  288.6 1.0 subtract_divide_fusion
  289.6 28.9 %reduce-scatter.2.cloned.1.call-done = bf16[128,1152]{1,0:T(8,128)(2,1)} async-done(((bf16[1024,1152]{1,0:T(8,128)(2,1)}), bf16[128,1152]{1,0:T(8,128)(2,1)}) %reduce-scatter.2.cloned.1.call-update) | async-done | bytes 294928 | tf_op jit(solution)/shard_map/reduce_scatter | solution.py:68
  318.5 1.2 fusion.6
  319.7 2.0 fusion.7
  (31 shorter events, 2.1 us)
Async XLA Ops:
  7.2 49.9 %all-gather.2.cloned.1.call-start = ((), (), s32[]{:S(2)}) async-start(), calls=%async_computation.1 | async-start | bytes 2654208 | tf_op jit(solution)/shard_map/all_gather | solution.py:50
  10.2 308.4 %reduce-scatter.2.cloned.1.call-start = ((), (), s32[]{:S(2)}) async-start(), calls=%async_computation.2 | async-start | bytes 2654208 | tf_op jit(solution)/shard_map/reduce_scatter | solution.py:68
  57.0 112.0 %collective-permute-start.1 = (bf16[1024,1152]{1,0:T(8,128)(2,1)}, bf16[1024,1152]{1,0:T(8,128)(2,1)S(1)}, u32[]{:S(2)}, u32[]{:S(2)}) collective-permute-start(bf16[1024,1152]{1,0:T(8,128)(2,1)} %all-gather.2.cloned.1.call-done), channel_id=1, source_target_pairs={{0,504},{8,0},{16,8},{24,16},{32,24},{40,32},{48,40},{56,48},{64,5... | collective-permute-start | bytes 7077896 | tf_op jit(solution)/shard_map/ppermute | solution.py:12
  68.0 149.9 %collective-permute-start = (bf16[1024,1152]{1,0:T(8,128)(2,1)}, bf16[1024,1152]{1,0:T(8,128)(2,1)S(1)}, u32[]{:S(2)}, u32[]{:S(2)}) collective-permute-start(bf16[1024,1152]{1,0:T(8,128)(2,1)} %all-gather.2.cloned.1.call-done), channel_id=1, source_target_pairs={{0,8},{8,16},{16,24},{24,32},{32,40},{40,48},{48,56},{56,64},{64,7... | collective-permute-start | bytes 7077896 | tf_op jit(solution)/shard_map/ppermute | solution.py:12
  169.1 2.4 copy-start.5
  169.1 2.4 copy-start.1
  172.3 109.6 %collective-permute-start.3 = (bf16[1024,1152]{1,0:T(8,128)(2,1)S(1)}, bf16[1024,1152]{1,0:T(8,128)(2,1)S(1)}, u32[]{:S(2)}, u32[]{:S(2)}) collective-permute-start(bf16[1024,1152]{1,0:T(8,128)(2,1)S(1)} %convolution_convert_fusion), channel_id=1, source_target_pairs={{0,8},{8,16},{16,24},{24,32},{32,40},{40,48},{48,56},{56,64},{64,7... | collective-permute-start | bytes 7077896 | tf_op jit(solution)/shard_map/ppermute | solution.py:12
  217.9 1.4 copy-start.3
  219.3 0.9 copy-start.9
  219.3 2.9 copy-start.2
  219.3 2.9 copy-start.7
  220.2 61.8 %collective-permute-start.2 = (bf16[1024,1152]{1,0:T(8,128)(2,1)S(1)}, bf16[1024,1152]{1,0:T(8,128)(2,1)S(1)}, u32[]{:S(2)}, u32[]{:S(2)}) collective-permute-start(bf16[1024,1152]{1,0:T(8,128)(2,1)S(1)} %convolution_convert_fusion.2), channel_id=1, source_target_pairs={{0,504},{8,0},{16,8},{24,16},{32,24},{40,32},{48,40},{56,48},{64,5... | collective-permute-start | bytes 7077896 | tf_op jit(solution)/shard_map/ppermute | solution.py:12
  223.4 0.9 copy-start.8
  284.3 2.3 copy-start.6
  286.1 1.7 copy-start.4
  286.1 1.7 copy-start.10
  287.9 30.7 %copy-start = (bf16[128,1152]{1,0:T(8,128)(2,1)S(1)}, bf16[128,1152]{1,0:T(8,128)(2,1)}, u32[]{:S(2)}) copy-start(bf16[128,1152]{1,0:T(8,128)(2,1)} %param.6) | copy-start | bytes 884740
Sparse Core Ops, SparseCore 0:
  10.7 46.3 all-gather.1
  284.4 34.0 reduce-scatter.1
where the time goes:
time: 330 us; the launch traced here: 329 us
  waiting for transfers between devices  274 us (83%)
  starting transfers between devices  17 us (5%)
  between operations  15.5 us (5%)
  other arithmetic  11.1 us (3%)
  matrix products  10.3 us (3%)
    ppermute x4, waiting for transfers between devices, from_behind(): return lax.ppermute(value, axis, pairs)  198 us
    all_gather x1, waiting for transfers between devices, per_device(): own_block = lax.all_gather(text_unit, 'group', axis=0, tiled=True)  46.8 us
    reduce_scatter x1, waiting for transfers between devices, per_device(): lax.psum_scatter(partial_value.astype(jnp.bfloat16), 'group', scatter_dim...  28.9 us
    ppermute x4, starting transfers between devices, from_behind(): return lax.ppermute(value, axis, pairs)  16.9 us
  transfers between devices with their start and end apart: 6, of which 5 were waited for; matrix products, arithmetic and copies ran while one was open for 4% of the time, Pallas kernels for 0%

commit v1 on v0

v1 whole, which is shorter than its diff:
```python
import jax
import jax.numpy as jnp
from jax import lax
from jax.sharding import PartitionSpec as P

EPSILON = 1e-06


def unit_rows(values):
    wide = values.astype(jnp.float32)
    length = jnp.sqrt(jnp.sum(wide * wide, axis=-1, keepdims=True) + EPSILON)
    return (wide / length, length)


def through_norm(sums, unit_float, length):
    return (sums - unit_float * jnp.sum(unit_float * sums, axis=-1, keepdims=True)) / length


def block_pairs(blocks, members):
    half = blocks // 2
    pairs = []
    for block in range(blocks):
        for member in range(members):
            partner = member
            if block % half == half - 1:
                chip, core = divmod(member, 2)
                partner = (members // 2 - 1 - chip) * 2 + core
            pairs.append((block * members + member, ((block + 1) % blocks) * members + partner))
    return pairs


def per_device(blocks, members, images, captions, labels, logit_scale, logit_bias):
    scale_value = logit_scale[0]
    bias_value = logit_bias[0]
    up = block_pairs(blocks, members)
    down = [(target, source) for source, target in up]
    image_float, image_length = unit_rows(images)
    image_unit = image_float.astype(jnp.bfloat16)
    text_float, text_length = unit_rows(captions)
    text_unit = text_float.astype(jnp.bfloat16)
    all_labels = lax.all_gather(labels, "group", axis=0, tiled=True)
    all_images = lax.all_gather(image_unit, "group", axis=0, tiled=True)
    lower = lax.ppermute(text_unit, ("blk", "group"), up)
    upper = lax.ppermute(text_unit, ("blk", "group"), down)
    texts = jnp.concatenate([text_unit, lower, upper], axis=0)
    raw = lax.dot_general(
        all_images, texts, (((1,), (1,)), ((), ())), preferred_element_type=jnp.float32
    )
    logits = scale_value * raw + bias_value
    rows = labels.shape[0]
    columns = lax.broadcasted_iota(jnp.int32, logits.shape, 1)
    wanted = all_labels - lax.axis_index("group") * rows
    positive = jnp.logical_and(columns < rows, columns == wanted[:, None])
    signed = jnp.where(positive, logits, -logits)
    row_loss = -jnp.sum(jax.nn.log_sigmoid(signed), axis=1)
    slope = jnp.where(positive, -1.0, 1.0) * jax.nn.sigmoid(-signed)
    weights = (scale_value * slope).astype(jnp.bfloat16)
    text_part = lax.dot_general(
        weights, all_images, (((0,), (0,)), ((), ())), preferred_element_type=jnp.float32
    )
    from_above = lax.ppermute(text_part[rows : 2 * rows].astype(jnp.bfloat16), ("blk", "group"), down)
    from_below = lax.ppermute(text_part[2 * rows :].astype(jnp.bfloat16), ("blk", "group"), up)
    image_part = jnp.dot(weights, texts, preferred_element_type=jnp.float32)
    image_sums = lax.psum_scatter(
        image_part.astype(jnp.bfloat16), "group", scatter_dimension=0, tiled=True
    ).astype(jnp.float32)
    loss_rows = lax.psum_scatter(row_loss, "group", scatter_dimension=0, tiled=True)
    text_sums = text_part[:rows] + from_above.astype(jnp.float32) + from_below.astype(jnp.float32)
    image_grad = through_norm(image_sums, image_float, image_length)
    text_grad = through_norm(text_sums, text_float, text_length)
    return (loss_rows, image_grad, text_grad)


def solution(mesh):
    blocks, members = mesh.shape["blk"], mesh.shape["group"]

    def body(*arrays):
        return per_device(blocks, members, *arrays)

    in_specs = (P(("blk", "group"), None), P(("blk", "group"), None), P(("blk", "group")), P(), P())
    out_specs = (P(("blk", "group")), P(("blk", "group"), None), P(("blk", "group"), None))
    return jax.shard_map(body, mesh=mesh, in_specs=in_specs, out_specs=out_specs, check_vma=False)
```

time: 330 us -> 128 us (0.39)
  waiting for transfers between devices: 274 us -> 22 us
  blocking collectives: 0 us -> 33.2 us
  starting transfers between devices: 17 us -> 32.8 us
    ppermute x4, waiting for transfers between devices: 198 us -> 0.01 us  [the longest x1 0.01 us: per_device(): lower = lax.ppermute(text_unit, ('blk', 'group'), up)]
    all_gather x1, waiting for transfers between devices: 46.8 us -> 15.4 us  [per_device(): all_images = lax.all_gather(image_unit, 'group', axis=0, tiled=True)]
    reduce_scatter x1, waiting for transfers between devices: 28.9 us -> 6.48 us  [per_device(): lax.psum_scatter(image_part.astype(jnp.bfloat16), 'group', scatter_dimens...]
    unnamed x0 -> x1, blocking collectives: none -> 17.8 us
    ppermute x4, starting transfers between devices: 16.9 us -> 32.7 us  [the longest x1 16.6 us: per_device(): upper = lax.ppermute(text_unit, ('blk', 'group'), down)]
    all_gather x0 -> x1, blocking collectives: none -> 15.4 us  [per_device(): all_labels = lax.all_gather(labels, 'group', axis=0, tiled=True)]
    dot_general x9 -> x3, matrix products: 10.3 us -> 10.9 us  [the longest x1 4 us: per_device(): lax.dot_general(all_images, texts, (((1,), (1,)), ((), ())), preferred_el...]
  transfers between devices with their start and end apart: 6 -> 6, of which waited for: 5 -> 2; matrix products, arithmetic and copies ran while one was open for 4% -> 7% of each run, Pallas kernels for 0% -> 0%
where the time goes in v1:
time: 128 us; the launch traced here: 127 us
  blocking collectives  33.2 us (26%)
  starting transfers between devices  32.8 us (26%)
  waiting for transfers between devices  22 us (17%)
  between operations  16.1 us (13%)
  matrix products  10.9 us (9%)
  other arithmetic  8.73 us (7%)
  local copies, waits for them, and re-layouts  3.08 us (2%)
    unnamed x1, blocking collectives  17.8 us
    ppermute x1, starting transfers between devices, per_device(): upper = lax.ppermute(text_unit, ('blk', 'group'), down)  16.6 us
    all_gather x1, waiting for transfers between devices, per_device(): all_images = lax.all_gather(image_unit, 'group', axis=0, tiled=True)  15.4 us
    all_gather x1, blocking collectives, per_device(): all_labels = lax.all_gather(labels, 'group', axis=0, tiled=True)  15.4 us
    ppermute x1, starting transfers between devices, per_device(): lax.ppermute(text_part[rows:2 * rows].astype(jnp.bfloat16), ('blk', 'grou...  12.2 us
    reduce_scatter x1, waiting for transfers between devices, per_device(): lax.psum_scatter(image_part.astype(jnp.bfloat16), 'group', scatter_dimens...  6.48 us
    dot_general x1, matrix products, per_device(): lax.dot_general(all_images, texts, (((1,), (1,)), ((), ())), preferred_el...  4 us
    dot_general x1, matrix products, per_device(): lax.dot_general(weights, all_images, (((0,), (0,)), ((), ())), preferred_...  3.77 us
  transfers between devices with their start and end apart: 6, of which 2 were waited for; matrix products, arithmetic and copies ran while one was open for 7% of the time, Pallas kernels for 0%

profile of v1, /device:TPU:1, one launch (start us, length us, event | category | flops | bytes accessed | tf_op | source)
XLA Modules:
  0.0 126.8 jit_solution(15195168764616297908)
XLA Ops:
  7.2 0.0 all-gather.3.cloned.1.call-start
  7.2 1.1 fusion.2
  8.4 1.8 %fusion.10 = bf16[128,1152]{1,0:T(8,128)(2,1)} fusion(f32[128]{0:T(128)S(1)} %add_sqrt_fusion.1, bf16[128,1152]{1,0:T(8,128)(2,1)} %param.5), kind=kLoop, calls=%fused_computation.29 | loop fusion | flops 442368 | bytes 590336 | tf_op jit(solution)/shard_map/convert_element_type | solution.py:38
  10.2 0.0 reduce-scatter.2.cloned.1.call-start
  10.3 1.1 fusion.3
  11.4 0.1 fusion.9
  11.5 16.6 %collective-permute-start.1 = (bf16[128,1152]{1,0:T(8,128)(2,1)S(1)}, bf16[128,1152]{1,0:T(8,128)(2,1)S(1)}, u32[]{:S(2)}, u32[]{:S(2)}) collective-permute-start(bf16[128,1152]{1,0:T(8,128)(2,1)S(1)} %fusion.9), channel_id=1, source_target_pairs={{8,0},{9,1},{10,2},{11,3},{12,4},{13,5},{14,6},{15,7},{16,8},{17,9... | collective-permute-start | bytes 884744 | tf_op jit(solution)/shard_map/ppermute | solution.py:44
  28.1 1.9 %collective-permute-start = (bf16[128,1152]{1,0:T(8,128)(2,1)S(1)}, bf16[128,1152]{1,0:T(8,128)(2,1)S(1)}, u32[]{:S(2)}, u32[]{:S(2)}) collective-permute-start(bf16[128,1152]{1,0:T(8,128)(2,1)S(1)} %fusion.9), channel_id=1, source_target_pairs={{0,8},{1,9},{2,10},{3,11},{4,12},{5,13},{6,14},{7,15},{8,16},{9,17... | collective-permute-start | bytes 884744 | tf_op jit(solution)/shard_map/ppermute | solution.py:43
  31.4 15.4 %all-gather = s32[8,1,128]{2,1,0:T(1,128)S(1)} all-gather(s32[1,1,128]{2,1,0:T(1,128)S(1)} %bitcast.17), channel_id=1, replica_groups=mesh['blk'=64,'group'=8] {'group'}, dimensions={0}, use_global_device_ids=true | all-gather | bytes 4608 | tf_op jit(solution)/shard_map/all_gather | solution.py:41
  46.7 15.4 %all-gather.3.cloned.1.call-done = bf16[1024,1152]{1,0:T(8,128)(2,1)} async-done(((bf16[128,1152]{1,0:T(8,128)(2,1)}), bf16[1024,1152]{1,0:T(8,128)(2,1)}) %all-gather.3.cloned.1.call-update) | async-done | bytes 2359312 | tf_op jit(solution)/shard_map/all_gather | solution.py:42
  62.2 4.0 %fusion = (f32[1024]{0:T(1024)S(1)}, f32[1024,384]{0,1:T(8,128)S(1)}) fusion(f32[]{:T(128)} %bitcast.12, bf16[1024,1152]{1,0:T(8,128)(2,1)} %all-gather.3.cloned.1.call-done, bf16[128,1152]{1,0:T(8,128)(2,1)S(1)} %collective-permute-done.1, bf16[128,1152]{1,0:T(8,128)(2,1)S(1)} %collective-permute-done, bf16[128,1152]{1,0:T(8,128)(2,1)S(1)} %fusion.9, ...), kind=kOutput, calls=%fused_computation.3 | convolution fusion | flops 914127872 | bytes 4825480 | tf_op jit(solution)/shard_map/dot_general | solution.py:46
  66.2 1.2 copy-done.3
  67.4 3.2 %convolution_convert_fusion = bf16[1024,1152]{1,0:T(8,128)(2,1)} fusion(bf16[128,1152]{1,0:T(8,128)(2,1)S(1)} %collective-permute-done.1, bf16[128,1152]{1,0:T(8,128)(2,1)S(1)} %collective-permute-done, bf16[128,1152]{1,0:T(8,128)(2,1)S(1)} %fusion.9, f32[1024,384]{0,1:T(8,128)S(1)} %get-tuple-element.6, f32[]{:T(128)} %bitcast.10, s32[1024]{0:T(1024)S(1)} %bitcast.15, ...), kind=kOutput, calls=%fused_computation.1 | convolution fusion | flops 912949248 | bytes 4821380 | tf_op jit(solution)/shard_map/dot_general | solution.py:63
  70.5 3.8 %fusion.13 = (bf16[384,1152]{1,0:T(8,128)(2,1)S(1)}, f32[384,1152]{1,0:T(8,128)S(1)}) fusion(bf16[1024,1152]{1,0:T(8,128)(2,1)} %all-gather.3.cloned.1.call-done, f32[1024,384]{0,1:T(8,128)} %copy-done.3, f32[]{:T(128)} %bitcast.11, s32[1024]{0:T(1024)S(1)} %bitcast.16, pred[384]{0:T(512)(128)(4,1)S(1)} %iota_compare_fusion.1), kind=kOutput, calls=%fused_computation.32 | convolution fusion | flops 909557760 | bytes 6590852 | tf_op jit(solution)/shard_map/dot_general | solution.py:58
  74.4 1.9 %collective-permute-start.3 = (bf16[128,1152]{1,0:T(8,128)(2,1)S(1)}, bf16[128,1152]{1,0:T(8,128)(2,1)S(1)}, u32[]{:S(2)}, u32[]{:S(2)}) collective-permute-start(bf16[128,1152]{1,0:T(8,128)(2,1)S(1)} %get-tuple-element.4), channel_id=1, source_target_pairs={{0,8},{1,9},{2,10},{3,11},{4,12},{5,13},{6,14},{7,15},{8,16},{9,17... | collective-permute-start | bytes 884744 | tf_op jit(solution)/shard_map/ppermute | solution.py:62
  76.3 12.2 %collective-permute-start.2 = (bf16[128,1152]{1,0:T(8,128)(2,1)S(1)}, bf16[128,1152]{1,0:T(8,128)(2,1)S(1)}, u32[]{:S(2)}, u32[]{:S(2)}) collective-permute-start(bf16[128,1152]{1,0:T(8,128)(2,1)S(1)} %get-tuple-element.3), channel_id=1, source_target_pairs={{8,0},{9,1},{10,2},{11,3},{12,4},{13,5},{14,6},{15,7},{16,8},{17,9... | collective-permute-start | bytes 884744 | tf_op jit(solution)/shard_map/ppermute | solution.py:61
  88.6 1.3 %dynamic-slice = u32[1]{0:T(128)} dynamic-slice(u32[512]{0:T(512)} %constant.24, u32[]{:T(128)S(6)} %add.49), dynamic_slice_sizes={1} | dynamic-slice | bytes 12
  90.5 17.8 %all-reduce = f32[1024]{0:T(1024)S(1)} all-reduce(f32[1024]{0:T(1024)S(1)} %get-tuple-element.5), channel_id=2, replica_groups=mesh['blk'=64,'group'=8] {'group'}, use_global_device_ids=true, to_apply=%region_3.4.clone | all-reduce | flops 1024 | bytes 8192
  108.3 0.6 dynamic-slice.1
  108.9 0.3 multiply_reduce_fusion
  109.2 1.1 subtract_divide_fusion
  110.3 6.5 %reduce-scatter.2.cloned.1.call-done = bf16[128,1152]{1,0:T(8,128)(2,1)} async-done(((bf16[1024,1152]{1,0:T(8,128)(2,1)}), bf16[128,1152]{1,0:T(8,128)(2,1)}) %reduce-scatter.2.cloned.1.call-update) | async-done | bytes 294928 | tf_op jit(solution)/shard_map/reduce_scatter | solution.py:64
  116.8 1.2 fusion.4
  118.0 2.0 %fusion.5 = f32[128,1152]{1,0:T(8,128)} fusion(bf16[128,1152]{1,0:T(8,128)(2,1)} %reduce-scatter.2.cloned.1.call-done, f32[128]{0:T(128)S(1)} %fusion.4, f32[128]{0:T(128)S(1)} %add_sqrt_fusion.1, bf16[128,1152]{1,0:T(8,128)(2,1)S(1)} %copy-done.1), kind=kLoop, calls=%fused_computation.17 | loop fusion | flops 884736 | bytes 1180672 | tf_op jit(solution)/shard_map/div | solution.py:16
  (18 shorter events, 0.1 us)
Async XLA Ops:
  7.2 4.2 %copy-start = (bf16[128,1152]{1,0:T(8,128)(2,1)S(1)}, bf16[128,1152]{1,0:T(8,128)(2,1)}, u32[]{:S(2)}) copy-start(bf16[128,1152]{1,0:T(8,128)(2,1)} %param.6) | copy-start | bytes 884740
  7.2 24.2 %copy-start.2 = (s32[128]{0:T(128)S(1)}, s32[128]{0:T(128)}, u32[]{:S(2)}) copy-start(s32[128]{0:T(128)} %param.7) | copy-start | bytes 1540
  7.2 55.0 %all-gather.3.cloned.1.call-start = ((), (), s32[]{:S(2)}) async-start(), calls=%async_computation.1 | async-start | bytes 2654208 | tf_op jit(solution)/shard_map/all_gather | solution.py:42
  10.2 106.5 %reduce-scatter.2.cloned.1.call-start = ((), (), s32[]{:S(2)}) async-start(), calls=%async_computation.2 | async-start | bytes 2654208 | tf_op jit(solution)/shard_map/reduce_scatter | solution.py:64
  11.5 35.2 %collective-permute-start.1 = (bf16[128,1152]{1,0:T(8,128)(2,1)S(1)}, bf16[128,1152]{1,0:T(8,128)(2,1)S(1)}, u32[]{:S(2)}, u32[]{:S(2)}) collective-permute-start(bf16[128,1152]{1,0:T(8,128)(2,1)S(1)} %fusion.9), channel_id=1, source_target_pairs={{8,0},{9,1},{10,2},{11,3},{12,4},{13,5},{14,6},{15,7},{16,8},{17,9... | collective-permute-start | bytes 884744 | tf_op jit(solution)/shard_map/ppermute | solution.py:44
  28.1 18.6 %collective-permute-start = (bf16[128,1152]{1,0:T(8,128)(2,1)S(1)}, bf16[128,1152]{1,0:T(8,128)(2,1)S(1)}, u32[]{:S(2)}, u32[]{:S(2)}) collective-permute-start(bf16[128,1152]{1,0:T(8,128)(2,1)S(1)} %fusion.9), channel_id=1, source_target_pairs={{0,8},{1,9},{2,10},{3,11},{4,12},{5,13},{6,14},{7,15},{8,16},{9,17... | collective-permute-start | bytes 884744 | tf_op jit(solution)/shard_map/ppermute | solution.py:43
  66.2 1.2 copy-start.3
  74.4 34.5 %collective-permute-start.3 = (bf16[128,1152]{1,0:T(8,128)(2,1)S(1)}, bf16[128,1152]{1,0:T(8,128)(2,1)S(1)}, u32[]{:S(2)}, u32[]{:S(2)}) collective-permute-start(bf16[128,1152]{1,0:T(8,128)(2,1)S(1)} %get-tuple-element.4), channel_id=1, source_target_pairs={{0,8},{1,9},{2,10},{3,11},{4,12},{5,13},{6,14},{7,15},{8,16},{9,17... | collective-permute-start | bytes 884744 | tf_op jit(solution)/shard_map/ppermute | solution.py:62
  76.3 32.6 %collective-permute-start.2 = (bf16[128,1152]{1,0:T(8,128)(2,1)S(1)}, bf16[128,1152]{1,0:T(8,128)(2,1)S(1)}, u32[]{:S(2)}, u32[]{:S(2)}) collective-permute-start(bf16[128,1152]{1,0:T(8,128)(2,1)S(1)} %get-tuple-element.3), channel_id=1, source_target_pairs={{8,0},{9,1},{10,2},{11,3},{12,4},{13,5},{14,6},{15,7},{16,8},{17,9... | collective-permute-start | bytes 884744 | tf_op jit(solution)/shard_map/ppermute | solution.py:61
  108.9 7.8 %copy-start.1 = (bf16[128,1152]{1,0:T(8,128)(2,1)S(1)}, bf16[128,1152]{1,0:T(8,128)(2,1)}, u32[]{:S(2)}) copy-start(bf16[128,1152]{1,0:T(8,128)(2,1)} %param.5) | copy-start | bytes 884740
Sparse Core Ops, SparseCore 0:
  10.7 51.4 all-gather.2
  70.7 46.0 reduce-scatter.1

commit v2 on v1

v2 whole, which is shorter than its diff:
```python
import functools

import jax
import jax.numpy as jnp
from jax import lax
from jax.experimental import pallas as pl
from jax.experimental.pallas import tpu as pltpu
from jax.sharding import PartitionSpec as P

EPSILON = 1e-06
CHIPS = 4
AG_CHUNKS = 2
RS_CHUNKS = 4
MESH = pl.DeviceIdType.MESH
F32 = jnp.float32
BF16 = jnp.bfloat16


def unit_rows(values):
    wide = values.astype(F32)
    length = jnp.sqrt(jnp.sum(wide * wide, axis=-1, keepdims=True) + EPSILON)
    return (wide / length, length)


def through_norm(sums, unit_float, length):
    return (sums - unit_float * jnp.sum(unit_float * sums, axis=-1, keepdims=True)) / length


def pair_weights(raw, positive, scale, bias):
    turned = scale * raw + bias
    if positive is not None:
        turned = jnp.where(positive, -turned, turned)
    decay = jnp.exp(-jnp.abs(turned))
    loss = jnp.maximum(turned, 0.0) + jnp.log1p(decay)
    share = jnp.where(turned >= 0, 1.0, decay) / (1.0 + decay)
    if positive is not None:
        share = jnp.where(positive, -share, share)
    return (jnp.sum(loss, axis=0, keepdims=True), (scale * share).astype(BF16))


def kernel(
    blocks,
    images,
    captions,
    labels,
    scale_ref,
    bias_ref,
    loss_out,
    image_out,
    text_out,
    imgs,
    texts,
    labs,
    loss_part,
    loss_in,
    parts,
    parts_out,
    parts_in,
    sums,
    sums_out,
    sums_in,
    back_out,
    back_in,
    ag_own_send,
    ag_fwd_send,
    ag_recv,
    lab_send,
    lab_recv,
    loss_send,
    loss_recv,
    core_send,
    core_recv,
    next_send,
    next_recv,
    rs_send,
    rs_recv,
    sum_send,
    sum_recv,
    back_send,
    back_recv,
):
    rows = images.shape[0]
    ag_rows = rows // AG_CHUNKS
    rs_rows = rows // RS_CHUNKS
    blk = lax.axis_index("blk")
    group = lax.axis_index("group")
    y = group // 2
    core = group % 2
    other = group + 1 - 2 * core
    half = blocks // 2
    mirror = 2 * (CHIPS - 1 - 2 * y)
    up_dev = {
        "blk": (blk + 1) % blocks,
        "group": group + ((blk % half) // (half - 1)) * mirror,
    }
    down_dev = {
        "blk": (blk + blocks - 1) % blocks,
        "group": group + ((half - 1 - blk % half) // (half - 1)) * mirror,
    }
    other_dev = {"blk": blk, "group": other}

    def chip(position):
        return {"blk": blk, "group": (position + CHIPS) % CHIPS * 2 + core}

    def remote(src, dst, send, recv, device):
        return pltpu.make_async_remote_copy(
            src_ref=src, dst_ref=dst, send_sem=send, recv_sem=recv, device_id=device, device_id_type=MESH
        )

    is_end = (y == 0) | (y == CHIPS - 1)
    is_middle = (y == 1) | (y == 2)

    barrier = pltpu.get_barrier_semaphore()
    for device in [up_dev, down_dev, other_dev] + [chip((y + d) % CHIPS) for d in (1, 2, 3)]:
        pl.semaphore_signal(barrier, inc=1, device_id=device, device_id_type=MESH)

    image_float, _ = unit_rows(images[...])
    imgs[y] = image_float.astype(BF16)
    text_float, _ = unit_rows(captions[...])
    texts[0:rows, :] = text_float.astype(BF16)
    labs[y] = labels[...]

    pl.semaphore_wait(barrier, 6)

    def own_copy(c, direction):
        part = imgs.at[y, pl.ds(c * ag_rows, ag_rows)]
        return remote(
            part, part, ag_own_send.at[direction, c], ag_recv.at[y, c], chip(y + 1 - 2 * direction)
        )

    def fwd_copy(s, c):
        part = imgs.at[s, pl.ds(c * ag_rows, ag_rows)]
        target = jnp.where(s < y, y + 1, y - 1)
        return remote(part, part, ag_fwd_send.at[s, c], ag_recv.at[s, c], chip(target))

    def slot(i):
        return texts.at[pl.ds(i * rows, rows)]

    next_up = remote(slot(0), slot(2), next_send.at[0], next_recv.at[0], up_dev)
    next_down = remote(slot(0), slot(4), next_send.at[1], next_recv.at[1], down_dev)
    core_copies = [
        remote(slot(2 * i), slot(2 * i + 1), core_send.at[i], core_recv.at[i], other_dev) for i in range(3)
    ]

    for c in range(AG_CHUNKS):

        @pl.when(y < CHIPS - 1)
        def _():
            own_copy(c, 0).start()

        @pl.when(y > 0)
        def _():
            own_copy(c, 1).start()

    next_up.start()
    next_down.start()
    core_copies[0].start()
    lab_copies = [
        remote(labs.at[y], labs.at[y], lab_send.at[d - 1], lab_recv.at[y], chip((y + d) % CHIPS))
        for d in (1, 2, 3)
    ]
    for copy in lab_copies:
        copy.start()

    next_up.wait_recv()
    core_copies[1].start()
    next_down.wait_recv()
    core_copies[2].start()
    for copy in core_copies:
        copy.wait_recv()

    scale = scale_ref[0]
    bias = bias_ref[0]

    def arrive(s):
        for c in range(AG_CHUNKS):
            fwd = fwd_copy(s, c)
            fwd.wait_recv()

            @pl.when(is_middle)
            def _():
                fwd.start()

        remote(labs.at[s], labs.at[s], lab_send.at[0], lab_recv.at[s], chip(y + 1)).wait_recv()

    def compute(s, first):
        image = imgs[s]
        label = labs[s]
        loss = None
        part = None
        for i in range(3):
            text = texts[2 * i * rows : 2 * (i + 1) * rows, :]
            raw = lax.dot_general(text, image, (((1,), (1,)), ((), ())), preferred_element_type=F32)
            positive = None
            if i == 0:
                index = lax.broadcasted_iota(jnp.int32, raw.shape, 0)
                column = jnp.where(index < rows, group * rows + index, other * rows + index - rows)
                positive = column == label
            loss_i, weights = pair_weights(raw, positive, scale, bias)
            part_i = lax.dot_general(
                weights, text, (((0,), (0,)), ((), ())), preferred_element_type=F32
            )
            sum_i = jnp.dot(weights, image, preferred_element_type=F32)
            where = pl.ds(2 * i * rows, 2 * rows)
            if first:
                sums[where, :] = sum_i
            else:
                sums[where, :] += sum_i
            loss = loss_i if i == 0 else loss + loss_i
            part = part_i if i == 0 else part + part_i
        parts[s] = part
        loss_part[s] = loss

    def rs_copy(t, c, direction):
        where = pl.ds(c * rs_rows, rs_rows)
        return remote(
            parts_out.at[t, where],
            parts_in.at[direction, t, where],
            rs_send.at[t, c],
            rs_recv.at[direction, t, c],
            chip(y + 1 - 2 * direction),
        )

    end_direction = y // (CHIPS - 1)
    compute(y, True)

    def step(k, carry):
        ascending = jnp.where((y == 1) & (k == 1), 0, k)
        s = jnp.where(y < 2, ascending, CHIPS - 1 - jnp.where((y == 2) & (k == 1), 0, k))

        @pl.when((k == 1) | (k == 3) | is_end)
        def _():
            arrive(s)

        @pl.when((k == 1) & is_middle)
        def _():
            arrive(jnp.where(y == 1, 2, 1))

        compute(s, False)

        @pl.when(is_end)
        def _():
            parts_out[s] = parts[s].astype(BF16)
            for c in range(RS_CHUNKS):
                rs_copy(s, c, end_direction).start()

        return carry

    lax.fori_loop(1, CHIPS, step, 0)

    loss_copies = [
        remote(
            loss_part.at[(y + d) % CHIPS],
            loss_in.at[y],
            loss_send.at[d - 1],
            loss_recv.at[y],
            chip((y + d) % CHIPS),
        )
        for d in (1, 2, 3)
    ]
    for copy in loss_copies:
        copy.start()

    sum_copies = [
        remote(sums_out.at[i], sums_in.at[i], sum_send.at[i], sum_recv.at[i], other_dev) for i in range(3)
    ]
    back_copies = [
        remote(back_out.at[0], back_in.at[1], back_send.at[0], back_recv.at[1], down_dev),
        remote(back_out.at[1], back_in.at[0], back_send.at[1], back_recv.at[0], up_dev),
    ]
    for i in (1, 2, 0):
        sums_out[i] = sums[(2 * i + 1) * rows : (2 * i + 2) * rows, :].astype(BF16)
        sum_copies[i].start()
    for i in (1, 2):
        sum_copies[i].wait_recv()
        total = sums[2 * i * rows : (2 * i + 1) * rows, :] + sums_in[i].astype(F32)
        back_out[i - 1] = total.astype(BF16)
        back_copies[i - 1].start()

    def pass_on(t, c, direction):
        copy = rs_copy(t, c, direction)
        where = pl.ds(c * rs_rows, rs_rows)
        copy.wait_recv()
        total = parts[t, where, :] + parts_in[direction, t, where, :].astype(F32)
        parts_out[t, where, :] = total.astype(BF16)
        copy.start()

    @pl.when(is_middle)
    def _():
        inner = 3 - y
        outer = jnp.where(y == 1, 0, 3)
        far = 3 - outer
        inward = y - 1
        outward = 2 - y

        def near(c, carry):
            pass_on(inner, c, inward)
            return carry

        lax.fori_loop(0, RS_CHUNKS, near, 0)

        def ends(c, carry):
            pass_on(far, c, inward)
            pass_on(outer, c, outward)
            return carry

        lax.fori_loop(0, RS_CHUNKS, ends, 0)

    sum_copies[0].wait_recv()
    text_sums = sums[0:rows, :] + sums_in[0].astype(F32)
    for i in range(2):
        back_copies[1 - i].wait_recv()
        text_sums = text_sums + back_in[i].astype(F32)
    text_float, text_length = unit_rows(captions[...])
    text_out[...] = through_norm(text_sums, text_float, text_length)

    loss_total = loss_part[y]
    for d in (1, 2, 3):
        s = (y + d) % CHIPS
        remote(loss_part.at[s], loss_in.at[s], loss_send.at[0], loss_recv.at[s], chip(y + 1)).wait_recv()
        loss_total = loss_total + loss_in[s]
    loss_out[...] = loss_total

    for direction in (0, 1):

        @pl.when((y > 0) if direction == 0 else (y < CHIPS - 1))
        def _():
            for c in range(RS_CHUNKS):
                rs_copy(y, c, direction).wait_recv()
            parts[y] += parts_in[direction, y].astype(F32)

    image_float, image_length = unit_rows(images[...])
    image_out[...] = through_norm(parts[y], image_float, image_length)

    for c in range(AG_CHUNKS):

        @pl.when(y < CHIPS - 1)
        def _():
            own_copy(c, 0).wait_send()

        @pl.when(y > 0)
        def _():
            own_copy(c, 1).wait_send()

    for d in (1, 2, 3):
        s = (y + d) % CHIPS

        @pl.when(is_middle)
        def _():
            for c in range(AG_CHUNKS):
                fwd_copy(s, c).wait_send()

        for c in range(RS_CHUNKS):
            rs_copy(s, c, 0).wait_send()
    for copy in [next_up, next_down] + core_copies + lab_copies + loss_copies + sum_copies + back_copies:
        copy.wait_send()


def per_device(blocks, images, captions, labels, logit_scale, logit_bias):
    rows, width = images.shape
    vmem = pl.BlockSpec(memory_space=pltpu.VMEM)
    smem = pl.BlockSpec(memory_space=pltpu.SMEM)
    dma = pltpu.SemaphoreType.DMA
    loss, image_grad, text_grad = pl.pallas_call(
        functools.partial(kernel, blocks),
        out_shape=[
            jax.ShapeDtypeStruct((1, rows), F32),
            jax.ShapeDtypeStruct((rows, width), F32),
            jax.ShapeDtypeStruct((rows, width), F32),
        ],
        in_specs=[vmem, vmem, vmem, smem, smem],
        out_specs=[vmem, vmem, vmem],
        scratch_shapes=[
            pltpu.VMEM((CHIPS, rows, width), BF16),
            pltpu.VMEM((6 * rows, width), BF16),
            pltpu.VMEM((CHIPS, 1, rows), jnp.int32),
            pltpu.VMEM((CHIPS, 1, rows), F32),
            pltpu.VMEM((CHIPS, 1, rows), F32),
            pltpu.VMEM((CHIPS, rows, width), F32),
            pltpu.VMEM((CHIPS, rows, width), BF16),
            pltpu.VMEM((2, CHIPS, rows, width), BF16),
            pltpu.VMEM((6 * rows, width), F32),
            pltpu.VMEM((3, rows, width), BF16),
            pltpu.VMEM((3, rows, width), BF16),
            pltpu.VMEM((2, rows, width), BF16),
            pltpu.VMEM((2, rows, width), BF16),
            dma((2, AG_CHUNKS)),
            dma((CHIPS, AG_CHUNKS)),
            dma((CHIPS, AG_CHUNKS)),
            dma((3,)),
            dma((CHIPS,)),
            dma((3,)),
            dma((CHIPS,)),
            dma((3,)),
            dma((3,)),
            dma((2,)),
            dma((2,)),
            dma((CHIPS, RS_CHUNKS)),
            dma((2, CHIPS, RS_CHUNKS)),
            dma((3,)),
            dma((3,)),
            dma((2,)),
            dma((2,)),
        ],
        compiler_params=pltpu.CompilerParams(
            collective_id=0, has_side_effects=True, vmem_limit_bytes=48 * 1024 * 1024
        ),
    )(images, captions, labels.reshape(1, rows), logit_scale, logit_bias)
    return (loss.reshape(rows), image_grad, text_grad)


def solution(mesh):
    body = functools.partial(per_device, mesh.shape["blk"])
    in_specs = (P(("blk", "group"), None), P(("blk", "group"), None), P(("blk", "group")), P(), P())
    out_specs = (P(("blk", "group")), P(("blk", "group"), None), P(("blk", "group"), None))
    return jax.shard_map(body, mesh=mesh, in_specs=in_specs, out_specs=out_specs, check_vma=False)
```

time: 128 us -> 85.3 us (0.67)
  Pallas kernels: 0 us -> 78.4 us
  blocking collectives: 33.2 us -> 0 us
  starting transfers between devices: 32.8 us -> 0 us
  waiting for transfers between devices: 22 us -> 0 us
  between operations: 16.1 us -> 1.94 us
  matrix products: 10.9 us -> 0 us
  other arithmetic: 8.73 us -> 0 us
  local copies, waits for them, and re-layouts: 3.08 us -> 4.71 us
    pallas_call x0 -> x1, Pallas kernels: none -> 78.4 us  [per_device(): pl.pallas_call(functools.partial(kernel, blocks), out_shape=[jax.ShapeDty...]
    ppermute x4 -> x0, starting transfers between devices: 32.7 us -> none  [the longest x1 16.6 us: per_device(): upper = lax.ppermute(text_unit, ('blk', 'group'), down)]
    unnamed x1 -> x0, blocking collectives: 17.8 us -> none
    all_gather x1 -> x0, waiting for transfers between devices: 15.4 us -> none  [per_device(): all_images = lax.all_gather(image_unit, 'group', axis=0, tiled=True)]
    all_gather x1 -> x0, blocking collectives: 15.4 us -> none  [per_device(): all_labels = lax.all_gather(labels, 'group', axis=0, tiled=True)]
    dot_general x3 -> x0, matrix products: 10.9 us -> none  [the longest x1 4 us: per_device(): lax.dot_general(all_images, texts, (((1,), (1,)), ((), ())), preferred_el...]
    reduce_scatter x1 -> x0, waiting for transfers between devices: 6.48 us -> none  [per_device(): lax.psum_scatter(image_part.astype(jnp.bfloat16), 'group', scatter_dimens...]
    reduce_sum x4 -> x0, other arithmetic: 3.73 us -> none  [the longest x2 2.24 us: unit_rows(): length = jnp.sqrt(jnp.sum(wide * wide, axis=-1, keepdims=True) + EPSILON)]
  transfers between devices with their start and end apart: 6 -> 0, of which waited for: 2 -> 0; matrix products, arithmetic and copies ran while one was open for 7% -> 0% of each run, Pallas kernels for 0% -> 0%
where the time goes in v2:
time: 85.3 us; the launch traced here: 85.1 us
  Pallas kernels  78.4 us (92%)
  local copies, waits for them, and re-layouts  4.71 us (6%)
  between operations  1.94 us (2%)
    pallas_call x1, Pallas kernels, per_device(): pl.pallas_call(functools.partial(kernel, blocks), out_shape=[jax.ShapeDty...  78.4 us
    unnamed x9, local copies, waits for them, and re-layouts  4.71 us

profile of v2, /device:TPU:1, one launch (start us, length us, event | category | flops | bytes accessed | tf_op | source)
XLA Modules:
  0.0 85.1 jit_solution(14623386980351869280)
XLA Ops:
  1.9 0.0 copy-start.2
  1.9 0.6 copy-done.2
  2.6 0.0 copy-start
  2.6 1.0 %copy-done = bf16[128,1152]{1,0:T(8,128)(2,1)S(1)} copy-done((bf16[128,1152]{1,0:T(8,128)(2,1)S(1)}, bf16[128,1152]{1,0:T(8,128)(2,1)}, u32[]{:S(2)}) %copy-start) | copy-done | bytes 294936
  3.5 0.0 copy-start.1
  3.5 1.0 %copy-done.1 = bf16[128,1152]{1,0:T(8,128)(2,1)S(1)} copy-done((bf16[128,1152]{1,0:T(8,128)(2,1)S(1)}, bf16[128,1152]{1,0:T(8,128)(2,1)}, u32[]{:S(2)}) %copy-start.1) | copy-done | bytes 294936
  4.5 78.4 %shard_map.76 = (f32[1,128]{1,0:T(1,128)S(1)}, f32[128,1152]{1,0:T(8,128)S(1)}, f32[128,1152]{1,0:T(8,128)S(1)}) custom-call(bf16[128,1152]{1,0:T(8,128)(2,1)S(1)} %copy-done, bf16[128,1152]{1,0:T(8,128)(2,1)S(1)} %copy-done.1, s32[1,128]{1,0:T(1,128)S(1)} %bitcast.2, f32[1]{0:T(128)S(6)} %copy.11.scale_ref, f32[1]{0:T(128)S(6)} %copy.12.bias_ref), custom_call_target="tpu_custom_call" | custom-call | tf_op jit(solution)/shard_map/pallas_call | solution.py:364
  82.9 0.5 copy.13
  83.4 0.8 copy.14
  84.2 0.8 copy.15
Async XLA Ops:
  1.9 0.7 copy-start.2
  2.6 1.0 %copy-start = (bf16[128,1152]{1,0:T(8,128)(2,1)S(1)}, bf16[128,1152]{1,0:T(8,128)(2,1)}, u32[]{:S(2)}) copy-start(bf16[128,1152]{1,0:T(8,128)(2,1)} %images.1) | copy-start | bytes 884740
  3.5 1.0 %copy-start.1 = (bf16[128,1152]{1,0:T(8,128)(2,1)S(1)}, bf16[128,1152]{1,0:T(8,128)(2,1)}, u32[]{:S(2)}) copy-start(bf16[128,1152]{1,0:T(8,128)(2,1)} %captions.1) | copy-start | bytes 884740

commit v3 on v2

v3 whole, which is shorter than its diff:
```python
import functools

import jax
import jax.numpy as jnp
from jax import lax
from jax.experimental import pallas as pl
from jax.experimental.pallas import tpu as pltpu
from jax.sharding import PartitionSpec as P

EPSILON = 1e-06
CHIPS = 4
LINE = 8
AG_CHUNKS = 2
RS_CHUNKS = 8
RELAY_CHUNKS = 2
MESH = pl.DeviceIdType.MESH
F32 = jnp.float32
BF16 = jnp.bfloat16


def unit_rows(values):
    wide = values.astype(F32)
    length = jnp.sqrt(jnp.sum(wide * wide, axis=-1, keepdims=True) + EPSILON)
    return (wide / length, length)


def through_norm(sums, unit_float, length):
    return (sums - unit_float * jnp.sum(unit_float * sums, axis=-1, keepdims=True)) / length


def depth_part(a, b, start, stop):
    return lax.dot_general(
        a[:, start:stop], b[:, start:stop], (((1,), (1,)), ((), ())), preferred_element_type=F32
    )


def summed_log(decay):
    pieces = [decay[i : i + 8, :] for i in range(0, decay.shape[0], 8)]
    while len(pieces) > 1:
        pieces = [a + b + a * b for a, b in zip(pieces[::2], pieces[1::2])]
    return jnp.sum(jnp.log1p(pieces[0]), axis=0, keepdims=True)


def pair_weights(raw, positive, scale, bias):
    logits = scale * raw + bias
    turned = jnp.where(positive, -logits, logits)
    decay = jnp.exp(-jnp.abs(turned))
    loss = jnp.sum(jnp.maximum(turned, 0.0), axis=0, keepdims=True) + summed_log(decay)
    share = jnp.where(turned >= 0, 1.0, decay) / (1.0 + decay)
    weights = jnp.where(positive, -scale, scale) * share
    return (loss, weights.astype(BF16))


def kernel(
    blocks,
    images_hbm,
    captions_hbm,
    labels_hbm,
    scale_ref,
    bias_ref,
    loss_out,
    image_out,
    text_out,
    images,
    captions,
    imgs,
    texts,
    labs,
    loss_part,
    loss_in,
    parts,
    parts_out,
    end_in,
    mid_in,
    sums,
    sums_out,
    sums_in,
    back_out,
    back_in,
    relay_in,
    load_sem,
    ag_own_send,
    ag_fwd_send,
    ag_recv,
    lab_send,
    lab_recv,
    loss_send,
    loss_recv,
    core_send,
    core_recv,
    next_send,
    next_recv,
    end_send,
    end_recv,
    mid_send,
    mid_recv,
    sum_send,
    sum_recv,
    back_send,
    back_recv,
    relay_src_send,
    relay_recv,
    relay_fwd_send,
):
    rows = images.shape[0]
    ag_rows = rows // AG_CHUNKS
    rs_rows = rows // RS_CHUNKS
    relay_rows = rows // RELAY_CHUNKS
    blk = lax.axis_index("blk")
    group = lax.axis_index("group")
    y = group // 2
    core = group % 2
    other = group + 1 - 2 * core
    half = blocks // 2
    mirrored = 2 * (CHIPS - 1 - y) + core
    up_edge = (blk % half) // (half - 1)
    down_edge = (half - 1 - blk % half) // (half - 1)
    up_dev = {"blk": (blk + 1) % blocks, "group": group + up_edge * (mirrored - group)}
    down_dev = {"blk": (blk + blocks - 1) % blocks, "group": group + down_edge * (mirrored - group)}
    on_up = jnp.where(blk % half == LINE - 1, 1, 0)
    on_down = jnp.where(blk % half == half - LINE, 1, 0)
    shift = half - LINE
    via_dev = {"blk": blk + shift * (down_edge - up_edge), "group": group}
    from_dev = {"blk": (blk + blocks + (shift + 1) * (up_edge - down_edge)) % blocks, "group": mirrored}
    source_dev = {"blk": blk + shift * (on_up - on_down), "group": group}
    target_dev = {"blk": (blk + blocks + (shift + 1) * (on_up - on_down)) % blocks, "group": mirrored}
    other_dev = {"blk": blk, "group": other}

    def chip(position):
        return {"blk": blk, "group": (position + CHIPS) % CHIPS * 2 + core}

    def remote(src, dst, send, recv, device):
        return pltpu.make_async_remote_copy(
            src_ref=src, dst_ref=dst, send_sem=send, recv_sem=recv, device_id=device, device_id_type=MESH
        )

    is_end = (y == 0) | (y == CHIPS - 1)
    is_middle = (y == 1) | (y == 2)
    relayed_up = is_middle & (up_edge == 1)
    relayed_down = is_middle & (down_edge == 1)
    relayed = is_middle & (up_edge + down_edge == 1)
    relays = is_middle & (on_up + on_down == 1)

    loads = [
        pltpu.make_async_copy(captions_hbm, captions, load_sem.at[0]),
        pltpu.make_async_copy(images_hbm, images, load_sem.at[1]),
        pltpu.make_async_copy(labels_hbm, labs.at[y], load_sem.at[2]),
    ]
    for load in loads:
        load.start()

    barrier = pltpu.get_barrier_semaphore()

    def greet(device):
        pl.semaphore_signal(barrier, inc=1, device_id=device, device_id_type=MESH)

    for device in [up_dev, down_dev, other_dev] + [chip(y + d) for d in (1, 2, 3)]:
        greet(device)

    @pl.when(relayed)
    def _():
        greet(via_dev)
        greet(from_dev)

    @pl.when(relays)
    def _():
        greet(source_dev)
        greet(target_dev)

    loads[0].wait()
    text_float, _ = unit_rows(captions[...])
    texts[0:rows, :] = text_float.astype(BF16)
    loads[1].wait()
    image_float, _ = unit_rows(images[...])
    imgs[y] = image_float.astype(BF16)
    loads[2].wait()

    relay_peers = 2 * ((y * (3 - y)) // 2) * (up_edge + down_edge + on_up + on_down)
    pl.semaphore_wait(barrier, 6 + relay_peers)

    def own_copy(c, direction):
        part = imgs.at[y, pl.ds(c * ag_rows, ag_rows)]
        return remote(
            part, part, ag_own_send.at[direction, c], ag_recv.at[y, c], chip(y + 1 - 2 * direction)
        )

    def fwd_copy(s, c):
        part = imgs.at[s, pl.ds(c * ag_rows, ag_rows)]
        target = jnp.where(s < y, y + 1, y - 1)
        return remote(part, part, ag_fwd_send.at[s, c], ag_recv.at[s, c], chip(target))

    def slot(i):
        return texts.at[pl.ds(i * rows, rows)]

    def relay_source(kind, source, c):
        where = pl.ds(c * relay_rows, relay_rows)
        return remote(
            source.at[where],
            relay_in.at[kind, where],
            relay_src_send.at[kind, c],
            relay_recv.at[kind, c],
            via_dev,
        )

    def relay_on(kind, target, start, sem, c):
        where = pl.ds(c * relay_rows, relay_rows)
        return remote(
            relay_in.at[kind, where],
            target.at[pl.ds(start + c * relay_rows, relay_rows)],
            relay_fwd_send.at[kind, c],
            sem,
            target_dev,
        )

    def captions_on(c):
        return relay_on(0, texts, (2 * on_up + 4 * on_down) * rows, next_recv.at[on_down], c)

    def sums_on(c):
        return relay_on(1, back_in.at[on_down], 0, back_recv.at[on_down], c)

    next_up = remote(slot(0), slot(2), next_send.at[0], next_recv.at[0], up_dev)
    next_down = remote(slot(0), slot(4), next_send.at[1], next_recv.at[1], down_dev)
    core_copies = [
        remote(slot(2 * i), slot(2 * i + 1), core_send.at[i], core_recv.at[i], other_dev) for i in range(3)
    ]
    lab_copies = [
        remote(labs.at[y], labs.at[y], lab_send.at[d - 1], lab_recv.at[y], chip(y + d)) for d in (1, 2, 3)
    ]

    @pl.when(relayed)
    def _():
        for c in range(RELAY_CHUNKS):
            relay_source(0, slot(0), c).start()

    for c in range(AG_CHUNKS):

        @pl.when(y < CHIPS - 1)
        def _():
            own_copy(c, 0).start()

        @pl.when(y > 0)
        def _():
            own_copy(c, 1).start()

    core_copies[0].start()

    @pl.when(jnp.logical_not(relayed_up))
    def _():
        next_up.start()

    @pl.when(jnp.logical_not(relayed_down))
    def _():
        next_down.start()

    for copy in lab_copies:
        copy.start()

    parts[...] = jnp.zeros_like(parts)
    sums[...] = jnp.zeros_like(sums)
    loss_part[...] = jnp.zeros_like(loss_part)

    near = jnp.where(y == 0, 1, jnp.where(y == 1, 0, jnp.where(y == 2, 3, 2)))
    next_near = jnp.where(y == 0, 2, jnp.where(y == 1, 2, 1))
    far = jnp.where(y < 2, 3, 0)

    def take(s, c):
        copy = fwd_copy(s, c)
        copy.wait_recv()

        @pl.when(is_middle)
        def _():
            copy.start()

    def take_labels(s):
        remote(labs.at[s], labs.at[s], lab_send.at[0], lab_recv.at[s], chip(y + 1)).wait_recv()

    scale = scale_ref[0]
    bias = bias_ref[0]

    def compute(s, i):
        image = imgs[s]
        where = pl.ds(pl.multiple_of(2 * i * rows, 2 * rows), 2 * rows)
        text = texts[where, :]
        raw = depth_part(text, image, 0, 512) + depth_part(text, image, 512, text.shape[1])
        label = labs[s]
        mine = label - group * rows
        theirs = label - other * rows
        theirs = jnp.where((theirs >= 0) & (theirs < rows), theirs + rows, -1)
        place = jnp.where((mine >= 0) & (mine < rows), mine, theirs)
        place = jnp.where(i == 0, place, -1)
        positive = lax.broadcasted_iota(jnp.int32, raw.shape, 0) == place
        loss, weights = pair_weights(raw, positive, scale, bias)
        sums[where, :] += jnp.dot(weights, image, preferred_element_type=F32)
        parts[s] += lax.dot_general(weights, text, (((0,), (0,)), ((), ())), preferred_element_type=F32)
        loss_part[s] += loss

    def end_copy(t, c):
        where = pl.ds(c * rs_rows, rs_rows)
        return remote(
            parts_out.at[t, where],
            end_in.at[t, where],
            end_send.at[t, c],
            end_recv.at[t, c],
            chip(1 + y // (CHIPS - 1)),
        )

    def mid_copy(t, c):
        where = pl.ds(c * rs_rows, rs_rows)
        sender = (y + 1) % 2
        return remote(
            parts_out.at[t, where], mid_in.at[sender, where], mid_send.at[t, c], mid_recv.at[sender, c], chip(t)
        )

    def sum_copy(i):
        return remote(sums_out.at[i], sums_in.at[i], sum_send.at[i], sum_recv.at[i], other_dev)

    def step(u, carry):
        s = jnp.where(u < 9, jnp.where((u == 0) | (u == 4) | (u == 5), y, jnp.where(u < 4, near, next_near)), far)
        i = jnp.where(u < 4, jnp.where(u == 0, 0, u - 1), jnp.where(u < 6, u - 3, u % 3))
        i = jnp.where(u > 8, (u + 1) % 3, i)

        @pl.when(u == 0)
        def _():
            core_copies[0].wait_recv()

        @pl.when((u == 1) & is_middle)
        def _():
            for c in range(AG_CHUNKS):
                take(near, c)
                take(next_near, c)

        @pl.when((u == 1) & relays)
        def _():
            for c in range(RELAY_CHUNKS):
                relay_source(0, slot(0), c).wait_recv()
                captions_on(c).start()

        @pl.when((u == 1) & is_end)
        def _():
            for c in range(AG_CHUNKS):
                take(near, c)

        @pl.when(u == 1)
        def _():
            for other_slot in (near, next_near, far):
                take_labels(other_slot)

        @pl.when((u == 2) & is_middle)
        def _():
            take(far, 0)

        @pl.when(u == 2)
        def _():
            next_up.wait_recv()
            core_copies[1].start()
            next_down.wait_recv()
            core_copies[2].start()

        @pl.when((u == 2) & is_middle)
        def _():
            for c in range(1, AG_CHUNKS):
                take(far, c)

        @pl.when(u == 2)
        def _():
            core_copies[1].wait_recv()
            core_copies[2].wait_recv()

        @pl.when((u == 6) & is_end)
        def _():
            for c in range(AG_CHUNKS):
                take(next_near, c)

        @pl.when((u == 9) & is_end)
        def _():
            for c in range(AG_CHUNKS):
                take(far, c)

        compute(s, i)

        @pl.when(u > 8)
        def _():
            start = pl.multiple_of((2 * i + 1) * rows, rows)
            sums_out[i] = sums[pl.ds(start, rows), :].astype(BF16)
            sum_copy(i).start()

        @pl.when(((u == 3) | (u == 8) | (u == 11)) & is_end)
        def _():
            parts_out[s] = parts[s].astype(BF16)
            for c in range(RS_CHUNKS):
                end_copy(s, c).start()

        return carry

    lax.fori_loop(0, 3 * CHIPS, step, 0)

    back_down = remote(back_out.at[0], back_in.at[1], back_send.at[0], back_recv.at[1], down_dev)
    back_up = remote(back_out.at[1], back_in.at[0], back_send.at[1], back_recv.at[0], up_dev)
    for i in (1, 2):
        sum_copy(i).wait_recv()
        total = sums[2 * i * rows : (2 * i + 1) * rows, :] + sums_in[i].astype(F32)
        back_out[i - 1] = total.astype(BF16)

        @pl.when(jnp.logical_not(relayed_down if i == 1 else relayed_up))
        def _():
            (back_down if i == 1 else back_up).start()

    @pl.when(relayed)
    def _():
        for c in range(RELAY_CHUNKS):
            relay_source(1, back_out.at[up_edge], c).start()

    loss_copies = [
        remote(
            loss_part.at[(y + d) % CHIPS], loss_in.at[y], loss_send.at[d - 1], loss_recv.at[y], chip(y + d)
        )
        for d in (1, 2, 3)
    ]
    for copy in loss_copies:
        copy.start()

    def pass_on(t, c):
        where = pl.ds(pl.multiple_of(c * rs_rows, rs_rows), rs_rows)
        end_copy(t, c).wait_recv()
        total = parts[t, where, :] + end_in[t, where, :].astype(F32)
        parts_out[t, where, :] = total.astype(BF16)
        mid_copy(t, c).start()

    @pl.when(is_middle)
    def _():
        parts_out[near] = parts[near].astype(BF16)
        for c in range(RS_CHUNKS):
            mid_copy(near, c).start()

        def inner(c, carry):
            pass_on(next_near, c)
            return carry

        lax.fori_loop(0, RS_CHUNKS, inner, 0)

        def outer(c, carry):
            pass_on(far, c)

            @pl.when(relays & (c % (RS_CHUNKS // RELAY_CHUNKS) == RS_CHUNKS // RELAY_CHUNKS - 1))
            def _():
                part = c // (RS_CHUNKS // RELAY_CHUNKS)
                relay_source(1, back_out.at[up_edge], part).wait_recv()
                sums_on(part).start()

            return carry

        lax.fori_loop(0, RS_CHUNKS, outer, 0)

    sum_copy(0).wait_recv()
    text_sums = sums[0:rows, :] + sums_in[0].astype(F32)
    back_down.wait_recv()
    text_sums = text_sums + back_in[1].astype(F32)
    back_up.wait_recv()
    text_sums = text_sums + back_in[0].astype(F32)
    text_float, text_length = unit_rows(captions[...])
    text_out[...] = through_norm(text_sums, text_float, text_length)

    loss_total = loss_part[y]
    for d in (1, 2, 3):
        s = (y + d) % CHIPS
        remote(loss_part.at[s], loss_in.at[s], loss_send.at[0], loss_recv.at[s], chip(y + 1)).wait_recv()
        loss_total = loss_total + loss_in[s]
    loss_out[...] = loss_total

    for sender in (0, 1):

        @pl.when(y != sender + 1)
        def _():
            for c in range(RS_CHUNKS):
                where = pl.ds(c * rs_rows, rs_rows)
                part = mid_in.at[sender, where]
                remote(part, part, mid_send.at[0, c], mid_recv.at[sender, c], chip(y + 1)).wait_recv()
            parts[y] += mid_in[sender].astype(F32)

    @pl.when(is_middle)
    def _():
        for c in range(RS_CHUNKS):
            end_copy(y, c).wait_recv()
        parts[y] += end_in[y].astype(F32)

    image_float, image_length = unit_rows(images[...])
    image_out[...] = through_norm(parts[y], image_float, image_length)

    for c in range(AG_CHUNKS):

        @pl.when(y < CHIPS - 1)
        def _():
            own_copy(c, 0).wait_send()

        @pl.when(y > 0)
        def _():
            own_copy(c, 1).wait_send()

    def sent(d, carry):
        s = (y + d) % CHIPS

        @pl.when(is_middle)
        def _():
            for c in range(AG_CHUNKS):
                fwd_copy(s, c).wait_send()
            for c in range(RS_CHUNKS):
                mid_copy(s, c).wait_send()

        @pl.when(is_end)
        def _():
            for c in range(RS_CHUNKS):
                end_copy(s, c).wait_send()

        return carry

    lax.fori_loop(1, CHIPS, sent, 0)

    @pl.when(jnp.logical_not(relayed_up))
    def _():
        next_up.wait_send()
        back_up.wait_send()

    @pl.when(jnp.logical_not(relayed_down))
    def _():
        next_down.wait_send()
        back_down.wait_send()

    @pl.when(relayed)
    def _():
        for c in range(RELAY_CHUNKS):
            relay_source(0, slot(0), c).wait_send()
            relay_source(1, back_out.at[up_edge], c).wait_send()

    @pl.when(relays)
    def _():
        for c in range(RELAY_CHUNKS):
            captions_on(c).wait_send()
            sums_on(c).wait_send()

    for copy in core_copies + lab_copies + loss_copies + [sum_copy(i) for i in range(3)]:
        copy.wait_send()


def per_device(blocks, images, captions, labels, logit_scale, logit_bias):
    rows, width = images.shape
    vmem = pl.BlockSpec(memory_space=pltpu.VMEM)
    smem = pl.BlockSpec(memory_space=pltpu.SMEM)
    hbm = pl.BlockSpec(memory_space=pl.ANY)
    dma = pltpu.SemaphoreType.DMA
    loss, image_grad, text_grad = pl.pallas_call(
        functools.partial(kernel, blocks),
        out_shape=[
            jax.ShapeDtypeStruct((1, rows), F32),
            jax.ShapeDtypeStruct((rows, width), F32),
            jax.ShapeDtypeStruct((rows, width), F32),
        ],
        in_specs=[hbm, hbm, hbm, smem, smem],
        out_specs=[vmem, vmem, vmem],
        scratch_shapes=[
            pltpu.VMEM((rows, width), BF16),
            pltpu.VMEM((rows, width), BF16),
            pltpu.VMEM((CHIPS, rows, width), BF16),
            pltpu.VMEM((6 * rows, width), BF16),
            pltpu.VMEM((CHIPS, 1, rows), jnp.int32),
            pltpu.VMEM((CHIPS, 1, rows), F32),
            pltpu.VMEM((CHIPS, 1, rows), F32),
            pltpu.VMEM((CHIPS, rows, width), F32),
            pltpu.VMEM((CHIPS, rows, width), BF16),
            pltpu.VMEM((CHIPS, rows, width), BF16),
            pltpu.VMEM((2, rows, width), BF16),
            pltpu.VMEM((6 * rows, width), F32),
            pltpu.VMEM((3, rows, width), BF16),
            pltpu.VMEM((3, rows, width), BF16),
            pltpu.VMEM((2, rows, width), BF16),
            pltpu.VMEM((2, rows, width), BF16),
            pltpu.VMEM((2, rows, width), BF16),
            dma((3,)),
            dma((2, AG_CHUNKS)),
            dma((CHIPS, AG_CHUNKS)),
            dma((CHIPS, AG_CHUNKS)),
            dma((3,)),
            dma((CHIPS,)),
            dma((3,)),
            dma((CHIPS,)),
            dma((3,)),
            dma((3,)),
            dma((2,)),
            dma((2,)),
            dma((CHIPS, RS_CHUNKS)),
            dma((CHIPS, RS_CHUNKS)),
            dma((CHIPS, RS_CHUNKS)),
            dma((2, RS_CHUNKS)),
            dma((3,)),
            dma((3,)),
            dma((2,)),
            dma((2,)),
            dma((2, RELAY_CHUNKS)),
            dma((2, RELAY_CHUNKS)),
            dma((2, RELAY_CHUNKS)),
        ],
        compiler_params=pltpu.CompilerParams(
            collective_id=0, has_side_effects=True, vmem_limit_bytes=48 * 1024 * 1024
        ),
    )(images, captions, labels.reshape(1, rows), logit_scale, logit_bias)
    return (loss.reshape(rows), image_grad, text_grad)


def solution(mesh):
    body = functools.partial(per_device, mesh.shape["blk"])
    in_specs = (P(("blk", "group"), None), P(("blk", "group"), None), P(("blk", "group")), P(), P())
    out_specs = (P(("blk", "group")), P(("blk", "group"), None), P(("blk", "group"), None))
    return jax.shard_map(body, mesh=mesh, in_specs=in_specs, out_specs=out_specs, check_vma=False)
```

time: 85.3 us -> 78 us (0.914)
  the two profiles are of different devices: /device:TPU:1 before, /device:TPU:8 now
where the time goes in v3:
time: 78 us; the launch traced here: 77.8 us
  Pallas kernels  71.2 us (91%)
  local copies, waits for them, and re-layouts  4.71 us (6%)
  between operations  1.94 us (2%)
    pallas_call x1, Pallas kernels, per_device(): pl.pallas_call(functools.partial(kernel, blocks), out_shape=[jax.ShapeDty...  71.2 us
    unnamed x9, local copies, waits for them, and re-layouts  4.71 us

profile of v3, /device:TPU:8, one launch (start us, length us, event | category | flops | bytes accessed | tf_op | source)
XLA Modules:
  0.0 77.8 jit_solution(9354059914562877035)
XLA Ops:
  1.9 0.0 copy-start.2
  1.9 0.6 copy-done.2
  2.6 0.0 copy-start
  2.6 1.0 %copy-done = bf16[128,1152]{1,0:T(8,128)(2,1)S(1)} copy-done((bf16[128,1152]{1,0:T(8,128)(2,1)S(1)}, bf16[128,1152]{1,0:T(8,128)(2,1)}, u32[]{:S(2)}) %copy-start) | copy-done | bytes 294936
  3.5 0.0 copy-start.1
  3.5 1.0 %copy-done.1 = bf16[128,1152]{1,0:T(8,128)(2,1)S(1)} copy-done((bf16[128,1152]{1,0:T(8,128)(2,1)S(1)}, bf16[128,1152]{1,0:T(8,128)(2,1)}, u32[]{:S(2)}) %copy-start.1) | copy-done | bytes 294936
  4.5 71.2 %shard_map.76 = (f32[1,128]{1,0:T(1,128)S(1)}, f32[128,1152]{1,0:T(8,128)S(1)}, f32[128,1152]{1,0:T(8,128)S(1)}) custom-call(bf16[128,1152]{1,0:T(8,128)(2,1)S(1)} %copy-done, bf16[128,1152]{1,0:T(8,128)(2,1)S(1)} %copy-done.1, s32[1,128]{1,0:T(1,128)S(1)} %bitcast.2, f32[1]{0:T(128)S(6)} %copy.11.scale_ref, f32[1]{0:T(128)S(6)} %copy.12.bias_ref), custom_call_target="tpu_custom_call" | custom-call | tf_op jit(solution)/shard_map/pallas_call | solution.py:550
  75.7 0.5 copy.13
  76.2 0.8 %copy.14 = f32[128,1152]{1,0:T(8,128)} copy(f32[128,1152]{1,0:T(8,128)S(1)} %get-tuple-element.13) | data formatting | bytes 1179648
  77.0 0.8 %copy.15 = f32[128,1152]{1,0:T(8,128)} copy(f32[128,1152]{1,0:T(8,128)S(1)} %get-tuple-element.14) | data formatting | bytes 1179648
Async XLA Ops:
  1.9 0.7 copy-start.2
  2.6 1.0 %copy-start = (bf16[128,1152]{1,0:T(8,128)(2,1)S(1)}, bf16[128,1152]{1,0:T(8,128)(2,1)}, u32[]{:S(2)}) copy-start(bf16[128,1152]{1,0:T(8,128)(2,1)} %images_hbm.1) | copy-start | bytes 884740
  3.5 1.0 %copy-start.1 = (bf16[128,1152]{1,0:T(8,128)(2,1)S(1)}, bf16[128,1152]{1,0:T(8,128)(2,1)}, u32[]{:S(2)}) copy-start(bf16[128,1152]{1,0:T(8,128)(2,1)} %captions_hbm.1) | copy-start | bytes 884740

commit v4 on v3

--- a/solution.py
+++ b/solution.py
@@ -101,6 +101,7 @@
     relay_src_send,
     relay_recv,
     relay_fwd_send,
+    ready,
 ):
     rows = images.shape[0]
     ag_rows = rows // AG_CHUNKS
@@ -117,13 +118,13 @@
     down_edge = (half - 1 - blk % half) // (half - 1)
     up_dev = {"blk": (blk + 1) % blocks, "group": group + up_edge * (mirrored - group)}
     down_dev = {"blk": (blk + blocks - 1) % blocks, "group": group + down_edge * (mirrored - group)}
-    on_up = jnp.where(blk % half == LINE - 1, 1, 0)
+    on_up = down_edge
     on_down = jnp.where(blk % half == half - LINE, 1, 0)
     shift = half - LINE
-    via_dev = {"blk": blk + shift * (down_edge - up_edge), "group": group}
-    from_dev = {"blk": (blk + blocks + (shift + 1) * (up_edge - down_edge)) % blocks, "group": mirrored}
-    source_dev = {"blk": blk + shift * (on_up - on_down), "group": group}
-    target_dev = {"blk": (blk + blocks + (shift + 1) * (on_up - on_down)) % blocks, "group": mirrored}
+    via_dev = {"blk": blk + shift * down_edge - (half - 1) * up_edge, "group": group}
+    from_dev = {"blk": (blk + shift + 1) % blocks, "group": mirrored}
+    source_dev = {"blk": blk + (half - 1) * on_up - shift * on_down, "group": group}
+    target_dev = {"blk": (blk + blocks + half * on_up - (shift + 1) * on_down) % blocks, "group": mirrored}
     other_dev = {"blk": blk, "group": other}
 
     def chip(position):
@@ -140,6 +141,10 @@
     relayed_down = is_middle & (down_edge == 1)
     relayed = is_middle & (up_edge + down_edge == 1)
     relays = is_middle & (on_up + on_down == 1)
+    is_first = blk % LINE == 0
+    is_last = blk % LINE == LINE - 1
+    not_first = jnp.logical_not(is_first)
+    not_last = jnp.logical_not(is_last)
 
     loads = [
         pltpu.make_async_copy(captions_hbm, captions, load_sem.at[0]),
@@ -154,13 +159,20 @@
     def greet(device):
         pl.semaphore_signal(barrier, inc=1, device_id=device, device_id_type=MESH)
 
-    for device in [up_dev, down_dev, other_dev] + [chip(y + d) for d in (1, 2, 3)]:
+    for device in [other_dev] + [chip(y + d) for d in (1, 2, 3)]:
         greet(device)
 
-    @pl.when(relayed)
+    @pl.when(not_last)
+    def _():
+        greet(up_dev)
+
+    @pl.when(is_first)
+    def _():
+        greet(down_dev)
+
+    @pl.when(relayed & is_first)
     def _():
         greet(via_dev)
-        greet(from_dev)
 
     @pl.when(relays)
     def _():
@@ -175,8 +187,25 @@
     imgs[y] = image_float.astype(BF16)
     loads[2].wait()
 
-    relay_peers = 2 * ((y * (3 - y)) // 2) * (up_edge + down_edge + on_up + on_down)
-    pl.semaphore_wait(barrier, 6 + relay_peers)
+    inner = (y * (3 - y)) // 2
+    peers = 4 + jnp.where(is_first, 0, 1) + jnp.where(is_last, 1, 0)
+    peers = peers + inner * (2 * (up_edge + down_edge) + on_down)
+    pl.semaphore_wait(barrier, peers)
+
+    def answer(index, device):
+        pl.semaphore_signal(ready.at[index], inc=1, device_id=device, device_id_type=MESH)
+
+    @pl.when(not_first)
+    def _():
+        answer(0, down_dev)
+
+    @pl.when(is_last)
+    def _():
+        answer(1, up_dev)
+
+    @pl.when(relayed & is_last)
+    def _():
+        answer(2, from_dev)
 
     def own_copy(c, direction):
         part = imgs.at[y, pl.ds(c * ag_rows, ag_rows)]
@@ -244,16 +273,20 @@
 
     core_copies[0].start()
 
-    @pl.when(jnp.logical_not(relayed_up))
-    def _():
-        next_up.start()
-
-    @pl.when(jnp.logical_not(relayed_down))
+    @pl.when(not_first)
     def _():
         next_down.start()
 
     for copy in lab_copies:
         copy.start()
+
+    @pl.when(not_last)
+    def _():
+        pl.semaphore_wait(ready.at[0], 1)
+
+    @pl.when(jnp.logical_not(relayed_up))
+    def _():
+        next_up.start()
 
     parts[...] = jnp.zeros_like(parts)
     sums[...] = jnp.zeros_like(sums)
@@ -314,10 +347,41 @@
     def sum_copy(i):
         return remote(sums_out.at[i], sums_in.at[i], sum_send.at[i], sum_recv.at[i], other_dev)
 
+    def finish(i):
+        sum_copy(i).wait_recv()
+        total = sums[2 * i * rows : (2 * i + 1) * rows, :] + sums_in[i].astype(F32)
+        back_out[i - 1] = total.astype(BF16)
+        direct = back_down if i == 1 else back_up
+        edge = relayed_down if i == 1 else relayed_up
+
+        @pl.when(jnp.logical_not(edge))
+        def _():
+            direct.start()
+
+        @pl.when(edge)
+        def _():
+            for c in range(RELAY_CHUNKS):
+                relay_source(1, back_out.at[i - 1], c).start()
+
+    back_down = remote(back_out.at[0], back_in.at[1], back_send.at[0], back_recv.at[1], down_dev)
+    back_up = remote(back_out.at[1], back_in.at[0], back_send.at[1], back_recv.at[0], up_dev)
+
+    def chosen(u, usual, first):
+        value = usual[0]
+        for k in range(len(usual)):
+            value = jnp.where(u == k, jnp.where(is_first, first[k], usual[k]), value)
+        return value
+
+    def pass_captions(c):
+        relay_source(0, slot(0), c).wait_recv()
+        captions_on(c).start()
+
+    usual_order = [y, near, near, near, y, y, next_near, next_near, next_near, far, far, far]
+    first_order = [y, near, near, y, next_near, next_near, far, far, far, next_near, near, y]
+
     def step(u, carry):
-        s = jnp.where(u < 9, jnp.where((u == 0) | (u == 4) | (u == 5), y, jnp.where(u < 4, near, next_near)), far)
-        i = jnp.where(u < 4, jnp.where(u == 0, 0, u - 1), jnp.where(u < 6, u - 3, u % 3))
-        i = jnp.where(u > 8, (u + 1) % 3, i)
+        s = chosen(u, usual_order, first_order)
+        i = chosen(u, [0, 0, 1, 2, 1, 2, 0, 1, 2, 2, 1, 0], [0, 0, 2, 2, 0, 2, 2, 0, 1, 1, 1, 1])
 
         @pl.when(u == 0)
         def _():
@@ -329,12 +393,6 @@
                 take(near, c)
                 take(next_near, c)
 
-        @pl.when((u == 1) & relays)
-        def _():
-            for c in range(RELAY_CHUNKS):
-                relay_source(0, slot(0), c).wait_recv()
-                captions_on(c).start()
-
         @pl.when((u == 1) & is_end)
         def _():
             for c in range(AG_CHUNKS):
@@ -345,46 +403,87 @@
             for other_slot in (near, next_near, far):
                 take_labels(other_slot)
 
-        @pl.when((u == 2) & is_middle)
-        def _():
-            take(far, 0)
-
-        @pl.when(u == 2)
+        @pl.when((u == 2) & is_first)
+        def _():
+            next_down.wait_recv()
+            core_copies[2].start()
+
+        @pl.when((u == 2) & not_first)
         def _():
             next_up.wait_recv()
             core_copies[1].start()
+
+        @pl.when((u == 2) & is_middle)
+        def _():
+            take(far, 0)
+
+        @pl.when((u == 2) & is_first)
+        def _():
+            core_copies[2].wait_recv()
+
+        @pl.when((u == 2) & not_first)
+        def _():
             next_down.wait_recv()
             core_copies[2].start()
-
-        @pl.when((u == 2) & is_middle)
+            core_copies[1].wait_recv()
+
+        @pl.when((u == 3) & not_first)
+        def _():
+            core_copies[2].wait_recv()
+
+        @pl.when((u == 4) & is_middle)
         def _():
             for c in range(1, AG_CHUNKS):
                 take(far, c)
 
-        @pl.when(u == 2)
-        def _():
-            core_copies[1].wait_recv()
-            core_copies[2].wait_recv()
-
-        @pl.when((u == 6) & is_end)
+        @pl.when((u == 4) & is_first)
+        def _():
+            pl.semaphore_wait(ready.at[1], 1)
+
+        @pl.when((u == 4) & is_first & jnp.logical_not(relayed_down))
+        def _():
+            next_down.start()
+
+        @pl.when((u == 4) & relays & (on_down == 1))
+        def _():
+            pl.semaphore_wait(ready.at[2], 1)
+            for c in range(RELAY_CHUNKS):
+                pass_captions(c)
+
+        @pl.when((u == jnp.where(is_first, 4, 6)) & is_end)
         def _():
             for c in range(AG_CHUNKS):
                 take(next_near, c)
 
-        @pl.when((u == 9) & is_end)
+        @pl.when((u == jnp.where(is_first, 6, 9)) & is_end)
         def _():
             for c in range(AG_CHUNKS):
                 take(far, c)
 
+        @pl.when((u == 8) & is_first)
+        def _():
+            finish(2)
+
+        @pl.when((u == 8) & relays & (on_up == 1))
+        def _():
+            for c in range(RELAY_CHUNKS):
+                pass_captions(c)
+
+        @pl.when((u == 8) & is_first)
+        def _():
+            next_up.wait_recv()
+            core_copies[1].start()
+            core_copies[1].wait_recv()
+
         compute(s, i)
 
-        @pl.when(u > 8)
+        @pl.when(jnp.where(is_first, (u == 6) | (u == 7) | (u == 11), u > 8))
         def _():
             start = pl.multiple_of((2 * i + 1) * rows, rows)
             sums_out[i] = sums[pl.ds(start, rows), :].astype(BF16)
             sum_copy(i).start()
 
-        @pl.when(((u == 3) | (u == 8) | (u == 11)) & is_end)
+        @pl.when(jnp.where(is_first, (u > 7) & (u < 11), (u == 3) | (u == 8) | (u == 11)) & is_end)
         def _():
             parts_out[s] = parts[s].astype(BF16)
             for c in range(RS_CHUNKS):
@@ -394,21 +493,11 @@
 
     lax.fori_loop(0, 3 * CHIPS, step, 0)
 
-    back_down = remote(back_out.at[0], back_in.at[1], back_send.at[0], back_recv.at[1], down_dev)
-    back_up = remote(back_out.at[1], back_in.at[0], back_send.at[1], back_recv.at[0], up_dev)
-    for i in (1, 2):
-        sum_copy(i).wait_recv()
-        total = sums[2 * i * rows : (2 * i + 1) * rows, :] + sums_in[i].astype(F32)
-        back_out[i - 1] = total.astype(BF16)
-
-        @pl.when(jnp.logical_not(relayed_down if i == 1 else relayed_up))
-        def _():
-            (back_down if i == 1 else back_up).start()
-
-    @pl.when(relayed)
-    def _():
-        for c in range(RELAY_CHUNKS):
-            relay_source(1, back_out.at[up_edge], c).start()
+    @pl.when(not_first)
+    def _():
+        finish(2)
+
+    finish(1)
 
     loss_copies = [
         remote(
@@ -419,6 +508,10 @@
     for copy in loss_copies:
         copy.start()
 
+    def pass_sums(c):
+        relay_source(1, back_out.at[up_edge], c).wait_recv()
+        sums_on(c).start()
+
     def pass_on(t, c):
         where = pl.ds(pl.multiple_of(c * rs_rows, rs_rows), rs_rows)
         end_copy(t, c).wait_recv()
@@ -432,24 +525,20 @@
         for c in range(RS_CHUNKS):
             mid_copy(near, c).start()
 
-        def inner(c, carry):
-            pass_on(next_near, c)
+        before = jnp.where(is_first, far, next_near)
+        after = jnp.where(is_first, next_near, far)
+
+        def pass_all(k, carry):
+            pass_on(jnp.where(k < RS_CHUNKS, before, after), k % RS_CHUNKS)
+
             return carry
 
-        lax.fori_loop(0, RS_CHUNKS, inner, 0)
-
-        def outer(c, carry):
-            pass_on(far, c)
-
-            @pl.when(relays & (c % (RS_CHUNKS // RELAY_CHUNKS) == RS_CHUNKS // RELAY_CHUNKS - 1))
-            def _():
-                part = c // (RS_CHUNKS // RELAY_CHUNKS)
-                relay_source(1, back_out.at[up_edge], part).wait_recv()
-                sums_on(part).start()
-
-            return carry
-
-        lax.fori_loop(0, RS_CHUNKS, outer, 0)
+        lax.fori_loop(0, 2 * RS_CHUNKS, pass_all, 0)
+
+    @pl.when(relays)
+    def _():
+        for c in range(RELAY_CHUNKS):
+            pass_sums(c)
 
     sum_copy(0).wait_recv()
     text_sums = sums[0:rows, :] + sums_in[0].astype(F32)
@@ -597,6 +686,7 @@
             dma((2, RELAY_CHUNKS)),
             dma((2, RELAY_CHUNKS)),
             dma((2, RELAY_CHUNKS)),
+            pltpu.SemaphoreType.REGULAR((3,)),
         ],
         compiler_params=pltpu.CompilerParams(
             collective_id=0, has_side_effects=True, vmem_limit_bytes=48 * 1024 * 1024

time: 78 us -> 72.3 us (0.927)
  the two profiles are of different devices: /device:TPU:8 before, /device:TPU:9 now
where the time goes in v4:
time: 72.3 us; the launch traced here: 72.1 us
  Pallas kernels  65.4 us (90%)
  local copies, waits for them, and re-layouts  4.71 us (7%)
  between operations  1.94 us (3%)
    pallas_call x1, Pallas kernels, per_device(): pl.pallas_call(functools.partial(kernel, blocks), out_shape=[jax.ShapeDty...  65.4 us
    unnamed x9, local copies, waits for them, and re-layouts  4.71 us

profile of v4, /device:TPU:9, one launch (start us, length us, event | category | flops | bytes accessed | tf_op | source)
XLA Modules:
  0.0 72.1 jit_solution(5199499097682642783)
XLA Ops:
  1.9 0.0 copy-start.2
  1.9 0.6 copy-done.2
  2.6 0.0 copy-start
  2.6 1.0 %copy-done = bf16[128,1152]{1,0:T(8,128)(2,1)S(1)} copy-done((bf16[128,1152]{1,0:T(8,128)(2,1)S(1)}, bf16[128,1152]{1,0:T(8,128)(2,1)}, u32[]{:S(2)}) %copy-start) | copy-done | bytes 294936
  3.5 0.0 copy-start.1
  3.5 1.0 %copy-done.1 = bf16[128,1152]{1,0:T(8,128)(2,1)S(1)} copy-done((bf16[128,1152]{1,0:T(8,128)(2,1)S(1)}, bf16[128,1152]{1,0:T(8,128)(2,1)}, u32[]{:S(2)}) %copy-start.1) | copy-done | bytes 294936
  4.5 65.4 %shard_map.76 = (f32[1,128]{1,0:T(1,128)S(1)}, f32[128,1152]{1,0:T(8,128)S(1)}, f32[128,1152]{1,0:T(8,128)S(1)}) custom-call(bf16[128,1152]{1,0:T(8,128)(2,1)S(1)} %copy-done, bf16[128,1152]{1,0:T(8,128)(2,1)S(1)} %copy-done.1, s32[1,128]{1,0:T(1,128)S(1)} %bitcast.2, f32[1]{0:T(128)S(6)} %copy.11.scale_ref, f32[1]{0:T(128)S(6)} %copy.12.bias_ref), custom_call_target="tpu_custom_call" | custom-call | tf_op jit(solution)/shard_map/pallas_call | solution.py:639
  69.9 0.5 copy.13
  70.4 0.8 %copy.14 = f32[128,1152]{1,0:T(8,128)} copy(f32[128,1152]{1,0:T(8,128)S(1)} %get-tuple-element.13) | data formatting | bytes 1179648
  71.3 0.8 %copy.15 = f32[128,1152]{1,0:T(8,128)} copy(f32[128,1152]{1,0:T(8,128)S(1)} %get-tuple-element.14) | data formatting | bytes 1179648
Async XLA Ops:
  1.9 0.7 copy-start.2
  2.6 1.0 %copy-start = (bf16[128,1152]{1,0:T(8,128)(2,1)S(1)}, bf16[128,1152]{1,0:T(8,128)(2,1)}, u32[]{:S(2)}) copy-start(bf16[128,1152]{1,0:T(8,128)(2,1)} %images_hbm.1) | copy-start | bytes 884740
  3.5 1.0 %copy-start.1 = (bf16[128,1152]{1,0:T(8,128)(2,1)S(1)}, bf16[128,1152]{1,0:T(8,128)(2,1)}, u32[]{:S(2)}) copy-start(bf16[128,1152]{1,0:T(8,128)(2,1)} %captions_hbm.1) | copy-start | bytes 884740

commit v5 on v4

--- a/solution.py
+++ b/solution.py
@@ -10,6 +10,7 @@
 EPSILON = 1e-06
 CHIPS = 4
 LINE = 8
+VIA = (24, 8)
 AG_CHUNKS = 2
 RS_CHUNKS = 8
 RELAY_CHUNKS = 2
@@ -118,13 +119,25 @@
     down_edge = (half - 1 - blk % half) // (half - 1)
     up_dev = {"blk": (blk + 1) % blocks, "group": group + up_edge * (mirrored - group)}
     down_dev = {"blk": (blk + blocks - 1) % blocks, "group": group + down_edge * (mirrored - group)}
-    on_up = down_edge
-    on_down = jnp.where(blk % half == half - LINE, 1, 0)
+    column = blk % half
     shift = half - LINE
-    via_dev = {"blk": blk + shift * down_edge - (half - 1) * up_edge, "group": group}
-    from_dev = {"blk": (blk + shift + 1) % blocks, "group": mirrored}
-    source_dev = {"blk": blk + (half - 1) * on_up - shift * on_down, "group": group}
-    target_dev = {"blk": (blk + blocks + half * on_up - (shift + 1) * on_down) % blocks, "group": mirrored}
+    passes = [jnp.where(column == offset, 1, 0) for offset in VIA]
+    on_down = passes[0] + passes[1]
+    on_up = jnp.where(column == LINE - 1, 1, 0)
+    offset = VIA[0] * passes[0] + VIA[1] * passes[1]
+
+    def inner_dev(step, turned=False):
+        return {"blk": (blk + 2 * blocks + step) % blocks, "group": mirrored if turned else group}
+
+    across_dev = inner_dev(half, True)
+    wrap_dev = inner_dev((half - 1) * (down_edge - up_edge))
+    via_devs = [inner_dev(v) for v in VIA]
+    from_devs = [inner_dev(1 + v, True) for v in VIA]
+    side_dev = inner_dev(shift * (on_up - up_edge))
+    late_from_dev = inner_dev(-(shift + 1), True)
+    late_to_dev = inner_dev(shift + 1, True)
+    caption_source_dev = inner_dev(-offset)
+    caption_target_dev = inner_dev(-(offset + 1), True)
     other_dev = {"blk": blk, "group": other}
 
     def chip(position):
@@ -141,6 +154,8 @@
     relayed_down = is_middle & (down_edge == 1)
     relayed = is_middle & (up_edge + down_edge == 1)
     relays = is_middle & (on_up + on_down == 1)
+    relays_down = is_middle & (on_down == 1)
+    relays_up = is_middle & (on_up == 1)
     is_first = blk % LINE == 0
     is_last = blk % LINE == LINE - 1
     not_first = jnp.logical_not(is_first)
@@ -170,14 +185,23 @@
     def _():
         greet(down_dev)
 
-    @pl.when(relayed & is_first)
-    def _():
-        greet(via_dev)
-
-    @pl.when(relays)
-    def _():
-        greet(source_dev)
-        greet(target_dev)
+    @pl.when(relayed)
+    def _():
+        greet(across_dev)
+
+    @pl.when(relayed_down)
+    def _():
+        for device in via_devs + [wrap_dev, late_from_dev]:
+            greet(device)
+
+    @pl.when(relayed_up | relays_up)
+    def _():
+        greet(side_dev)
+
+    @pl.when(relays_down)
+    def _():
+        greet(caption_source_dev)
+        greet(caption_target_dev)
 
     loads[0].wait()
     text_float, _ = unit_rows(captions[...])
@@ -189,7 +213,7 @@
 
     inner = (y * (3 - y)) // 2
     peers = 4 + jnp.where(is_first, 0, 1) + jnp.where(is_last, 1, 0)
-    peers = peers + inner * (2 * (up_edge + down_edge) + on_down)
+    peers = peers + inner * (5 * up_edge + 3 * down_edge + on_down + 2 * on_up)
     pl.semaphore_wait(barrier, peers)
 
     def answer(index, device):
@@ -205,7 +229,9 @@
 
     @pl.when(relayed & is_last)
     def _():
-        answer(2, from_dev)
+        for device in from_devs:
+            answer(2, device)
+        answer(3, wrap_dev)
 
     def own_copy(c, direction):
         part = imgs.at[y, pl.ds(c * ag_rows, ag_rows)]
@@ -221,31 +247,74 @@
     def slot(i):
         return texts.at[pl.ds(i * rows, rows)]
 
-    def relay_source(kind, source, c):
+    def relay_first(kind, source, c, device):
         where = pl.ds(c * relay_rows, relay_rows)
         return remote(
             source.at[where],
             relay_in.at[kind, where],
             relay_src_send.at[kind, c],
             relay_recv.at[kind, c],
-            via_dev,
+            device,
         )
 
-    def relay_on(kind, target, start, sem, c):
-        where = pl.ds(c * relay_rows, relay_rows)
+    def relay_on(kind, target, start, sem, c, device):
         return remote(
-            relay_in.at[kind, where],
+            relay_in.at[kind, pl.ds(c * relay_rows, relay_rows)],
             target.at[pl.ds(start + c * relay_rows, relay_rows)],
             relay_fwd_send.at[kind, c],
             sem,
-            target_dev,
+            device,
         )
 
+    def captions_first(c):
+        return [relay_first(0, slot(0), c, device) for device in (wrap_dev, via_devs[c])]
+
+    def sums_first(c):
+        up = relay_first(1, back_out.at[1], c, side_dev)
+        if c == 0:
+            half_rows = pl.ds(0, relay_rows)
+            up = remote(
+                back_out.at[1, half_rows],
+                back_in.at[0, half_rows],
+                relay_src_send.at[1, c],
+                back_recv.at[0],
+                up_dev,
+            )
+        return [up, relay_first(1, back_out.at[0], c, wrap_dev)]
+
     def captions_on(c):
-        return relay_on(0, texts, (2 * on_up + 4 * on_down) * rows, next_recv.at[on_down], c)
+        return [
+            relay_on(0, texts, 2 * rows, next_recv.at[0], c, across_dev),
+            relay_on(0, texts, 4 * rows, next_recv.at[1], c, caption_target_dev),
+        ]
 
     def sums_on(c):
-        return relay_on(1, back_in.at[on_down], 0, back_recv.at[on_down], c)
+        return [
+            relay_on(1, back_in.at[0], 0, back_recv.at[0], c, late_to_dev),
+            relay_on(1, back_in.at[1], 0, back_recv.at[1], c, across_dev),
+        ]
+
+    def each(copies, conditions, act):
+        for copy, condition in zip(copies, conditions):
+            pl.when(condition)(functools.partial(act, copy))
+
+    def start(copy):
+        copy.start()
+
+    def sent(copy):
+        copy.wait_send()
+
+    def arrived_start(pair):
+        pair[0].wait_recv()
+        pair[1].start()
+
+    def pass_captions(c):
+        ways = [(captions_first(c)[0], copy) for copy in captions_on(c)]
+        each(ways, (relayed_down, is_middle & (passes[c] == 1)), arrived_start)
+
+    def pass_sums(c):
+        ways = [(sums_first(c)[1], copy) for copy in sums_on(c)]
+        each(ways[c == 0 :], (relays_up, relayed_up)[c == 0 :], arrived_start)
 
     next_up = remote(slot(0), slot(2), next_send.at[0], next_recv.at[0], up_dev)
     next_down = remote(slot(0), slot(4), next_send.at[1], next_recv.at[1], down_dev)
@@ -256,10 +325,8 @@
         remote(labs.at[y], labs.at[y], lab_send.at[d - 1], lab_recv.at[y], chip(y + d)) for d in (1, 2, 3)
     ]
 
-    @pl.when(relayed)
-    def _():
-        for c in range(RELAY_CHUNKS):
-            relay_source(0, slot(0), c).start()
+    for c in range(RELAY_CHUNKS):
+        each(captions_first(c), (relayed_up, relayed_down), start)
 
     for c in range(AG_CHUNKS):
 
@@ -360,28 +427,28 @@
 
         @pl.when(edge)
         def _():
+            if i == 1:
+                pl.semaphore_wait(ready.at[3], 1)
             for c in range(RELAY_CHUNKS):
-                relay_source(1, back_out.at[i - 1], c).start()
+                sums_first(c)[2 - i].start()
 
     back_down = remote(back_out.at[0], back_in.at[1], back_send.at[0], back_recv.at[1], down_dev)
     back_up = remote(back_out.at[1], back_in.at[0], back_send.at[1], back_recv.at[0], up_dev)
 
-    def chosen(u, usual, first):
+    def chosen(u, usual, first, late):
         value = usual[0]
         for k in range(len(usual)):
             value = jnp.where(u == k, jnp.where(is_first, first[k], usual[k]), value)
+            value = jnp.where((u == k) & relayed_up, late[k], value)
         return value
 
-    def pass_captions(c):
-        relay_source(0, slot(0), c).wait_recv()
-        captions_on(c).start()
-
     usual_order = [y, near, near, near, y, y, next_near, next_near, next_near, far, far, far]
+    late_order = [y, near, near, y, next_near, next_near, near, y, next_near, far, far, far]
     first_order = [y, near, near, y, next_near, next_near, far, far, far, next_near, near, y]
 
     def step(u, carry):
-        s = chosen(u, usual_order, first_order)
-        i = chosen(u, [0, 0, 1, 2, 1, 2, 0, 1, 2, 2, 1, 0], [0, 0, 2, 2, 0, 2, 2, 0, 1, 1, 1, 1])
+        s = chosen(u, usual_order, first_order, late_order)
+        i = chosen(u, [0, 0, 1, 2, 1, 2, 0, 1, 2, 2, 1, 0], [0, 0, 2, 2, 0, 2, 2, 0, 1, 1, 1, 1], [0, 0, 1, 1, 0, 1, 2, 2, 2, 2, 1, 0])
 
         @pl.when(u == 0)
         def _():
@@ -405,51 +472,54 @@
 
         @pl.when((u == 2) & is_first)
         def _():
-            next_down.wait_recv()
-            core_copies[2].start()
-
-        @pl.when((u == 2) & not_first)
-        def _():
-            next_up.wait_recv()
-            core_copies[1].start()
-
-        @pl.when((u == 2) & is_middle)
-        def _():
-            take(far, 0)
-
-        @pl.when((u == 2) & is_first)
-        def _():
-            core_copies[2].wait_recv()
-
-        @pl.when((u == 2) & not_first)
-        def _():
-            next_down.wait_recv()
-            core_copies[2].start()
-            core_copies[1].wait_recv()
-
-        @pl.when((u == 3) & not_first)
-        def _():
-            core_copies[2].wait_recv()
-
-        @pl.when((u == 4) & is_middle)
-        def _():
-            for c in range(1, AG_CHUNKS):
-                take(far, c)
-
-        @pl.when((u == 4) & is_first)
-        def _():
             pl.semaphore_wait(ready.at[1], 1)
 
-        @pl.when((u == 4) & is_first & jnp.logical_not(relayed_down))
+        @pl.when((u == 2) & is_first & jnp.logical_not(relayed_down))
         def _():
             next_down.start()
 
-        @pl.when((u == 4) & relays & (on_down == 1))
+        @pl.when((u == 2) & relays_down)
         def _():
             pl.semaphore_wait(ready.at[2], 1)
             for c in range(RELAY_CHUNKS):
                 pass_captions(c)
 
+        @pl.when((u == 2) & is_first)
+        def _():
+            next_down.wait_recv()
+            core_copies[2].start()
+
+        @pl.when((u == 2) & not_first)
+        def _():
+            next_up.wait_recv()
+            core_copies[1].start()
+
+        @pl.when((u == 2) & is_middle)
+        def _():
+            take(far, 0)
+
+        @pl.when((u == 2) & is_first)
+        def _():
+            core_copies[2].wait_recv()
+
+        @pl.when((u == jnp.where(relayed_up, 6, 2)) & not_first)
+        def _():
+            next_down.wait_recv()
+            core_copies[2].start()
+
+        @pl.when((u == 2) & not_first)
+        def _():
+            core_copies[1].wait_recv()
+
+        @pl.when((u == jnp.where(relayed_up, 6, 3)) & not_first)
+        def _():
+            core_copies[2].wait_recv()
+
+        @pl.when((u == 4) & is_middle)
+        def _():
+            for c in range(1, AG_CHUNKS):
+                take(far, c)
+
         @pl.when((u == jnp.where(is_first, 4, 6)) & is_end)
         def _():
             for c in range(AG_CHUNKS):
@@ -460,13 +530,10 @@
             for c in range(AG_CHUNKS):
                 take(far, c)
 
-        @pl.when((u == 8) & is_first)
-        def _():
-            finish(2)
-
-        @pl.when((u == 8) & relays & (on_up == 1))
-        def _():
-            for c in range(RELAY_CHUNKS):
+        for c in range(RELAY_CHUNKS):
+
+            @pl.when((u == 6 + 2 * c) & relayed_down)
+            def _():
                 pass_captions(c)
 
         @pl.when((u == 8) & is_first)
@@ -475,7 +542,17 @@
             core_copies[1].start()
             core_copies[1].wait_recv()
 
+        @pl.when((u == 9) & is_first)
+        def _():
+            finish(2)
+
         compute(s, i)
+
+        @pl.when((u == jnp.where(is_first, 10, 9)) & is_middle)
+        def _():
+            parts_out[near] = parts[near].astype(BF16)
+            for c in range(RS_CHUNKS):
+                mid_copy(near, c).start()
 
         @pl.when(jnp.where(is_first, (u == 6) | (u == 7) | (u == 11), u > 8))
         def _():
@@ -508,10 +585,6 @@
     for copy in loss_copies:
         copy.start()
 
-    def pass_sums(c):
-        relay_source(1, back_out.at[up_edge], c).wait_recv()
-        sums_on(c).start()
-
     def pass_on(t, c):
         where = pl.ds(pl.multiple_of(c * rs_rows, rs_rows), rs_rows)
         end_copy(t, c).wait_recv()
@@ -521,21 +594,22 @@
 
     @pl.when(is_middle)
     def _():
-        parts_out[near] = parts[near].astype(BF16)
-        for c in range(RS_CHUNKS):
-            mid_copy(near, c).start()
-
         before = jnp.where(is_first, far, next_near)
         after = jnp.where(is_first, next_near, far)
 
         def pass_all(k, carry):
             pass_on(jnp.where(k < RS_CHUNKS, before, after), k % RS_CHUNKS)
+            for c in range(RELAY_CHUNKS):
+
+                @pl.when(relays_up & (k == RS_CHUNKS))
+                def _():
+                    pass_sums(c)
 
             return carry
 
         lax.fori_loop(0, 2 * RS_CHUNKS, pass_all, 0)
 
-    @pl.when(relays)
+    @pl.when(relayed_up)
     def _():
         for c in range(RELAY_CHUNKS):
             pass_sums(c)
@@ -585,7 +659,7 @@
         def _():
             own_copy(c, 1).wait_send()
 
-    def sent(d, carry):
+    def line_sent(d, carry):
         s = (y + d) % CHIPS
 
         @pl.when(is_middle)
@@ -602,7 +676,7 @@
 
         return carry
 
-    lax.fori_loop(1, CHIPS, sent, 0)
+    lax.fori_loop(1, CHIPS, line_sent, 0)
 
     @pl.when(jnp.logical_not(relayed_up))
     def _():
@@ -614,17 +688,10 @@
         next_down.wait_send()
         back_down.wait_send()
 
-    @pl.when(relayed)
-    def _():
-        for c in range(RELAY_CHUNKS):
-            relay_source(0, slot(0), c).wait_send()
-            relay_source(1, back_out.at[up_edge], c).wait_send()
-
-    @pl.when(relays)
-    def _():
-        for c in range(RELAY_CHUNKS):
-            captions_on(c).wait_send()
-            sums_on(c).wait_send()
+    for c in range(RELAY_CHUNKS):
+        each(captions_first(c) + sums_first(c), (relayed_up, relayed_down) * 2, sent)
+        each(captions_on(c), (relayed_down, is_middle & (passes[c] == 1)), sent)
+        each(sums_on(c)[c == 0 :], (relays_up, relayed_up)[c == 0 :], sent)
 
     for copy in core_copies + lab_copies + loss_copies + [sum_copy(i) for i in range(3)]:
         copy.wait_send()
@@ -686,7 +753,7 @@
             dma((2, RELAY_CHUNKS)),
             dma((2, RELAY_CHUNKS)),
             dma((2, RELAY_CHUNKS)),
-            pltpu.SemaphoreType.REGULAR((3,)),
+            pltpu.SemaphoreType.REGULAR((4,)),
         ],
         compiler_params=pltpu.CompilerParams(
             collective_id=0, has_side_effects=True, vmem_limit_bytes=48 * 1024 * 1024

time: 72.3 us -> 65.8 us (0.910)
  the two profiles are of different devices: /device:TPU:9 before, /device:TPU:1 now
where the time goes in v5:
time: 65.8 us; the launch traced here: 64.6 us
  Pallas kernels  58 us (88%)
  local copies, waits for them, and re-layouts  4.71 us (7%)
  between operations  1.94 us (3%)
    pallas_call x1, Pallas kernels, per_device(): pl.pallas_call(functools.partial(kernel, blocks), out_shape=[jax.ShapeDty...  58 us
    unnamed x9, local copies, waits for them, and re-layouts  4.71 us

profile of v5, /device:TPU:1, one launch (start us, length us, event | category | flops | bytes accessed | tf_op | source)
XLA Modules:
  0.0 64.6 jit_solution(780901984094237757)
XLA Ops:
  1.9 0.0 copy-start.2
  1.9 0.6 %copy-done.2 = s32[128]{0:T(128)S(1)} copy-done((s32[128]{0:T(128)S(1)}, s32[128]{0:T(128)}, u32[]{:S(2)}) %copy-start.2) | copy-done | bytes 536
  2.6 0.0 copy-start
  2.6 1.0 %copy-done = bf16[128,1152]{1,0:T(8,128)(2,1)S(1)} copy-done((bf16[128,1152]{1,0:T(8,128)(2,1)S(1)}, bf16[128,1152]{1,0:T(8,128)(2,1)}, u32[]{:S(2)}) %copy-start) | copy-done | bytes 294936
  3.5 0.0 copy-start.1
  3.5 1.0 %copy-done.1 = bf16[128,1152]{1,0:T(8,128)(2,1)S(1)} copy-done((bf16[128,1152]{1,0:T(8,128)(2,1)S(1)}, bf16[128,1152]{1,0:T(8,128)(2,1)}, u32[]{:S(2)}) %copy-start.1) | copy-done | bytes 294936
  4.5 58.0 %shard_map.76 = (f32[1,128]{1,0:T(1,128)S(1)}, f32[128,1152]{1,0:T(8,128)S(1)}, f32[128,1152]{1,0:T(8,128)S(1)}) custom-call(bf16[128,1152]{1,0:T(8,128)(2,1)S(1)} %copy-done, bf16[128,1152]{1,0:T(8,128)(2,1)S(1)} %copy-done.1, s32[1,128]{1,0:T(1,128)S(1)} %bitcast.2, f32[1]{0:T(128)S(6)} %copy.11.scale_ref, f32[1]{0:T(128)S(6)} %copy.12.bias_ref), custom_call_target="tpu_custom_call" | custom-call | tf_op jit(solution)/shard_map/pallas_call | solution.py:706
  62.5 0.5 copy.13
  63.0 0.8 %copy.14 = f32[128,1152]{1,0:T(8,128)} copy(f32[128,1152]{1,0:T(8,128)S(1)} %get-tuple-element.13) | data formatting | bytes 1179648
  63.8 0.8 %copy.15 = f32[128,1152]{1,0:T(8,128)} copy(f32[128,1152]{1,0:T(8,128)S(1)} %get-tuple-element.14) | data formatting | bytes 1179648
Async XLA Ops:
  1.9 0.7 %copy-start.2 = (s32[128]{0:T(128)S(1)}, s32[128]{0:T(128)}, u32[]{:S(2)}) copy-start(s32[128]{0:T(128)} %param.7) | copy-start | bytes 1540
  2.6 1.0 %copy-start = (bf16[128,1152]{1,0:T(8,128)(2,1)S(1)}, bf16[128,1152]{1,0:T(8,128)(2,1)}, u32[]{:S(2)}) copy-start(bf16[128,1152]{1,0:T(8,128)(2,1)} %images_hbm.1) | copy-start | bytes 884740
  3.5 1.0 %copy-start.1 = (bf16[128,1152]{1,0:T(8,128)(2,1)S(1)}, bf16[128,1152]{1,0:T(8,128)(2,1)}, u32[]{:S(2)}) copy-start(bf16[128,1152]{1,0:T(8,128)(2,1)} %captions_hbm.1) | copy-start | bytes 884740

commit v6 on v5

--- a/solution.py
+++ b/solution.py
@@ -10,10 +10,12 @@
 EPSILON = 1e-06
 CHIPS = 4
 LINE = 8
-VIA = (24, 8)
+CAPTIONS_VIA = ((24, 0, 48), (8, 48, 48), (16, 96, 32))
+CAPTIONS_UP_VIA = (8, 16)
+SUMS_UP_VIA = (24, 16)
+SUMS_DOWN_VIA = (23, 31)
 AG_CHUNKS = 2
 RS_CHUNKS = 8
-RELAY_CHUNKS = 2
 MESH = pl.DeviceIdType.MESH
 F32 = jnp.float32
 BF16 = jnp.bfloat16
@@ -107,7 +109,6 @@
     rows = images.shape[0]
     ag_rows = rows // AG_CHUNKS
     rs_rows = rows // RS_CHUNKS
-    relay_rows = rows // RELAY_CHUNKS
     blk = lax.axis_index("blk")
     group = lax.axis_index("group")
     y = group // 2
@@ -120,24 +121,12 @@
     up_dev = {"blk": (blk + 1) % blocks, "group": group + up_edge * (mirrored - group)}
     down_dev = {"blk": (blk + blocks - 1) % blocks, "group": group + down_edge * (mirrored - group)}
     column = blk % half
-    shift = half - LINE
-    passes = [jnp.where(column == offset, 1, 0) for offset in VIA]
-    on_down = passes[0] + passes[1]
-    on_up = jnp.where(column == LINE - 1, 1, 0)
-    offset = VIA[0] * passes[0] + VIA[1] * passes[1]
 
     def inner_dev(step, turned=False):
         return {"blk": (blk + 2 * blocks + step) % blocks, "group": mirrored if turned else group}
 
     across_dev = inner_dev(half, True)
     wrap_dev = inner_dev((half - 1) * (down_edge - up_edge))
-    via_devs = [inner_dev(v) for v in VIA]
-    from_devs = [inner_dev(1 + v, True) for v in VIA]
-    side_dev = inner_dev(shift * (on_up - up_edge))
-    late_from_dev = inner_dev(-(shift + 1), True)
-    late_to_dev = inner_dev(shift + 1, True)
-    caption_source_dev = inner_dev(-offset)
-    caption_target_dev = inner_dev(-(offset + 1), True)
     other_dev = {"blk": blk, "group": other}
 
     def chip(position):
@@ -153,9 +142,7 @@
     relayed_up = is_middle & (up_edge == 1)
     relayed_down = is_middle & (down_edge == 1)
     relayed = is_middle & (up_edge + down_edge == 1)
-    relays = is_middle & (on_up + on_down == 1)
-    relays_down = is_middle & (on_down == 1)
-    relays_up = is_middle & (on_up == 1)
+    in_column = {offset: is_middle & (column == offset) for offset in (7, 8, 15, 16, 23, 24)}
     is_first = blk % LINE == 0
     is_last = blk % LINE == LINE - 1
     not_first = jnp.logical_not(is_first)
@@ -185,23 +172,47 @@
     def _():
         greet(down_dev)
 
-    @pl.when(relayed)
+    @pl.when(relayed_down)
+    def _():
+        greet(wrap_dev)
+        for offset in CAPTIONS_UP_VIA:
+            greet(inner_dev(offset - half, True))
+        greet(inner_dev(SUMS_DOWN_VIA[0]))
+        for offset, _, _ in CAPTIONS_VIA:
+            greet(inner_dev(offset))
+        for offset in SUMS_UP_VIA:
+            greet(inner_dev(-offset - 1, True))
+
+    for offset in CAPTIONS_UP_VIA:
+
+        @pl.when(in_column[offset])
+        def _():
+            greet(inner_dev(half - 1 - offset))
+            greet(inner_dev(half - offset, True))
+
+    @pl.when(relayed_up)
     def _():
         greet(across_dev)
-
-    @pl.when(relayed_down)
-    def _():
-        for device in via_devs + [wrap_dev, late_from_dev]:
-            greet(device)
-
-    @pl.when(relayed_up | relays_up)
-    def _():
-        greet(side_dev)
-
-    @pl.when(relays_down)
-    def _():
-        greet(caption_source_dev)
-        greet(caption_target_dev)
+        greet(inner_dev(SUMS_DOWN_VIA[0] + 1 - blocks, True))
+        for offset in SUMS_UP_VIA:
+            greet(inner_dev(-offset))
+
+    for offset, _, _ in CAPTIONS_VIA:
+
+        @pl.when(in_column[offset])
+        def _():
+            greet(inner_dev(-offset))
+            greet(inner_dev(-offset - 1, True))
+
+    for offset in SUMS_UP_VIA:
+
+        @pl.when(in_column[half - 1 - offset])
+        def _():
+            greet(inner_dev(offset))
+
+    @pl.when(in_column[SUMS_DOWN_VIA[0]])
+    def _():
+        greet(inner_dev(blocks - 1 - SUMS_DOWN_VIA[0], True))
 
     loads[0].wait()
     text_float, _ = unit_rows(captions[...])
@@ -213,7 +224,10 @@
 
     inner = (y * (3 - y)) // 2
     peers = 4 + jnp.where(is_first, 0, 1) + jnp.where(is_last, 1, 0)
-    peers = peers + inner * (5 * up_edge + 3 * down_edge + on_down + 2 * on_up)
+    inner_peers = 10 * up_edge + 5 * down_edge
+    for offset, count in ((24, 1), (8, 2), (16, 2), (7, 2), (15, 2), (23, 2)):
+        inner_peers = inner_peers + jnp.where(column == offset, count, 0)
+    peers = peers + inner * inner_peers
     pl.semaphore_wait(barrier, peers)
 
     def answer(index, device):
@@ -229,9 +243,13 @@
 
     @pl.when(relayed & is_last)
     def _():
-        for device in from_devs:
-            answer(2, device)
-        answer(3, wrap_dev)
+        for offset, _, _ in CAPTIONS_VIA:
+            answer(2, inner_dev(offset + 1, True))
+        answer(4, wrap_dev)
+
+    @pl.when(in_column[SUMS_DOWN_VIA[0]])
+    def _():
+        answer(3, inner_dev(-SUMS_DOWN_VIA[0]))
 
     def own_copy(c, direction):
         part = imgs.at[y, pl.ds(c * ag_rows, ag_rows)]
@@ -247,74 +265,53 @@
     def slot(i):
         return texts.at[pl.ds(i * rows, rows)]
 
-    def relay_first(kind, source, c, device):
-        where = pl.ds(c * relay_rows, relay_rows)
-        return remote(
-            source.at[where],
-            relay_in.at[kind, where],
-            relay_src_send.at[kind, c],
-            relay_recv.at[kind, c],
-            device,
+    def flow(kind, c):
+        if kind == 0:
+            offset = CAPTIONS_UP_VIA[c]
+            begin, size, source = c * 64, 64, slot(0)
+            near_dev, far_dev = inner_dev(offset + 1 - half), inner_dev(half - offset, True)
+            target, base, sem, sends, passes = texts, 2 * rows, next_recv.at[0], relayed_up, in_column[offset]
+        elif kind == 1:
+            offset, begin, size = CAPTIONS_VIA[c]
+            source, near_dev, far_dev = slot(0), inner_dev(offset), inner_dev(-offset - 1, True)
+            target, base, sem, sends, passes = texts, 4 * rows, next_recv.at[1], relayed_down, in_column[offset]
+        elif kind == 2:
+            offset = SUMS_UP_VIA[c]
+            begin, size, source = c * 64, 64, back_out.at[1]
+            near_dev, far_dev = inner_dev(-offset), inner_dev(offset + 1, True)
+            target, base, sem = back_in.at[0], 0, back_recv.at[0]
+            sends, passes = relayed_up, in_column[half - 1 - offset]
+        else:
+            offset = SUMS_DOWN_VIA[c]
+            begin, size, source = c * 64, 64, back_out.at[0]
+            near_dev, far_dev = inner_dev(offset), inner_dev(blocks - 1 - offset, True)
+            target, base, sem = back_in.at[1], 0, back_recv.at[1]
+            sends, passes = relayed_down, in_column[offset] if c == 0 else relayed_up
+        held = relay_in.at[kind, pl.ds(begin, size)]
+        first = remote(
+            source.at[pl.ds(begin, size)], held, relay_src_send.at[kind, c], relay_recv.at[kind, c], near_dev
         )
-
-    def relay_on(kind, target, start, sem, c, device):
-        return remote(
-            relay_in.at[kind, pl.ds(c * relay_rows, relay_rows)],
-            target.at[pl.ds(start + c * relay_rows, relay_rows)],
-            relay_fwd_send.at[kind, c],
-            sem,
-            device,
+        second = remote(
+            held, target.at[pl.ds(base + begin, size)], relay_fwd_send.at[kind, c], sem, far_dev
         )
-
-    def captions_first(c):
-        return [relay_first(0, slot(0), c, device) for device in (wrap_dev, via_devs[c])]
-
-    def sums_first(c):
-        up = relay_first(1, back_out.at[1], c, side_dev)
-        if c == 0:
-            half_rows = pl.ds(0, relay_rows)
-            up = remote(
-                back_out.at[1, half_rows],
-                back_in.at[0, half_rows],
-                relay_src_send.at[1, c],
-                back_recv.at[0],
-                up_dev,
-            )
-        return [up, relay_first(1, back_out.at[0], c, wrap_dev)]
-
-    def captions_on(c):
-        return [
-            relay_on(0, texts, 2 * rows, next_recv.at[0], c, across_dev),
-            relay_on(0, texts, 4 * rows, next_recv.at[1], c, caption_target_dev),
-        ]
-
-    def sums_on(c):
-        return [
-            relay_on(1, back_in.at[0], 0, back_recv.at[0], c, late_to_dev),
-            relay_on(1, back_in.at[1], 0, back_recv.at[1], c, across_dev),
-        ]
-
-    def each(copies, conditions, act):
-        for copy, condition in zip(copies, conditions):
-            pl.when(condition)(functools.partial(act, copy))
-
-    def start(copy):
-        copy.start()
-
-    def sent(copy):
-        copy.wait_send()
-
-    def arrived_start(pair):
-        pair[0].wait_recv()
-        pair[1].start()
-
-    def pass_captions(c):
-        ways = [(captions_first(c)[0], copy) for copy in captions_on(c)]
-        each(ways, (relayed_down, is_middle & (passes[c] == 1)), arrived_start)
-
-    def pass_sums(c):
-        ways = [(sums_first(c)[1], copy) for copy in sums_on(c)]
-        each(ways[c == 0 :], (relays_up, relayed_up)[c == 0 :], arrived_start)
+        return first, second, sends, passes
+
+    flow_parts = [(0, 0), (0, 1), (1, 0), (1, 1), (1, 2), (2, 0), (2, 1), (3, 0), (3, 1)]
+
+    def send_flow(kind, c):
+        first, _, sends, _ = flow(kind, c)
+
+        @pl.when(sends)
+        def _():
+            first.start()
+
+    def pass_flow(kind, c):
+        first, second, _, passes = flow(kind, c)
+
+        @pl.when(passes)
+        def _():
+            first.wait_recv()
+            second.start()
 
     next_up = remote(slot(0), slot(2), next_send.at[0], next_recv.at[0], up_dev)
     next_down = remote(slot(0), slot(4), next_send.at[1], next_recv.at[1], down_dev)
@@ -325,8 +322,8 @@
         remote(labs.at[y], labs.at[y], lab_send.at[d - 1], lab_recv.at[y], chip(y + d)) for d in (1, 2, 3)
     ]
 
-    for c in range(RELAY_CHUNKS):
-        each(captions_first(c), (relayed_up, relayed_down), start)
+    for kind, c in flow_parts[:5]:
+        send_flow(kind, c)
 
     for c in range(AG_CHUNKS):
 
@@ -425,30 +422,38 @@
         def _():
             direct.start()
 
-        @pl.when(edge)
-        def _():
-            if i == 1:
+        if i == 1:
+
+            @pl.when(edge)
+            def _():
                 pl.semaphore_wait(ready.at[3], 1)
-            for c in range(RELAY_CHUNKS):
-                sums_first(c)[2 - i].start()
+                pl.semaphore_wait(ready.at[4], 1)
+
+        for c in range(2):
+            send_flow(4 - i, c)
 
     back_down = remote(back_out.at[0], back_in.at[1], back_send.at[0], back_recv.at[1], down_dev)
     back_up = remote(back_out.at[1], back_in.at[0], back_send.at[1], back_recv.at[0], up_dev)
 
-    def chosen(u, usual, first, late):
+    first_ends = is_first & is_end
+    end_step = jnp.where(is_end, 1, 0)
+
+    def chosen(u, usual, first, first_end, late):
         value = usual[0]
         for k in range(len(usual)):
             value = jnp.where(u == k, jnp.where(is_first, first[k], usual[k]), value)
             value = jnp.where((u == k) & relayed_up, late[k], value)
+            value = jnp.where((u == k) & first_ends, first_end[k], value)
         return value
 
     usual_order = [y, near, near, near, y, y, next_near, next_near, next_near, far, far, far]
     late_order = [y, near, near, y, next_near, next_near, near, y, next_near, far, far, far]
+    first_end_order = [y, near, near, y, next_near, next_near, next_near, far, far, far, near, y]
     first_order = [y, near, near, y, next_near, next_near, far, far, far, next_near, near, y]
 
     def step(u, carry):
-        s = chosen(u, usual_order, first_order, late_order)
-        i = chosen(u, [0, 0, 1, 2, 1, 2, 0, 1, 2, 2, 1, 0], [0, 0, 2, 2, 0, 2, 2, 0, 1, 1, 1, 1], [0, 0, 1, 1, 0, 1, 2, 2, 2, 2, 1, 0])
+        s = chosen(u, usual_order, first_order, first_end_order, late_order)
+        i = chosen(u, [0, 0, 1, 2, 1, 2, 0, 1, 2, 2, 1, 0], [0, 0, 2, 2, 0, 2, 2, 0, 1, 1, 1, 1], [0, 0, 2, 2, 0, 2, 1, 2, 0, 1, 1, 1], [0, 0, 1, 1, 0, 1, 2, 2, 2, 2, 1, 0])
 
         @pl.when(u == 0)
         def _():
@@ -478,11 +483,11 @@
         def _():
             next_down.start()
 
-        @pl.when((u == 2) & relays_down)
+        @pl.when((u == 2) & (in_column[8] | in_column[16] | in_column[24]))
         def _():
             pl.semaphore_wait(ready.at[2], 1)
-            for c in range(RELAY_CHUNKS):
-                pass_captions(c)
+            for c in range(3):
+                pass_flow(1, c)
 
         @pl.when((u == 2) & is_first)
         def _():
@@ -525,24 +530,23 @@
             for c in range(AG_CHUNKS):
                 take(next_near, c)
 
-        @pl.when((u == jnp.where(is_first, 6, 9)) & is_end)
+        @pl.when((u == jnp.where(is_first, 7, 9)) & is_end)
         def _():
             for c in range(AG_CHUNKS):
                 take(far, c)
 
-        for c in range(RELAY_CHUNKS):
-
-            @pl.when((u == 6 + 2 * c) & relayed_down)
-            def _():
-                pass_captions(c)
-
-        @pl.when((u == 8) & is_first)
+        @pl.when((u == 6) & (in_column[8] | in_column[16]))
+        def _():
+            pass_flow(0, 0)
+            pass_flow(0, 1)
+
+        @pl.when((u == jnp.where(is_end, 6, 8)) & is_first)
         def _():
             next_up.wait_recv()
             core_copies[1].start()
             core_copies[1].wait_recv()
 
-        @pl.when((u == 9) & is_first)
+        @pl.when((u == jnp.where(is_end, 11, 9)) & is_first)
         def _():
             finish(2)
 
@@ -554,13 +558,13 @@
             for c in range(RS_CHUNKS):
                 mid_copy(near, c).start()
 
-        @pl.when(jnp.where(is_first, (u == 6) | (u == 7) | (u == 11), u > 8))
+        @pl.when(jnp.where(is_first, (u == 6 + end_step) | (u == 7 + end_step) | (u == 11), u > 8))
         def _():
             start = pl.multiple_of((2 * i + 1) * rows, rows)
             sums_out[i] = sums[pl.ds(start, rows), :].astype(BF16)
             sum_copy(i).start()
 
-        @pl.when(jnp.where(is_first, (u > 7) & (u < 11), (u == 3) | (u == 8) | (u == 11)) & is_end)
+        @pl.when(jnp.where(is_first, (u == 6) | (u == 9) | (u == 10), (u == 3) | (u == 8) | (u == 11)) & is_end)
         def _():
             parts_out[s] = parts[s].astype(BF16)
             for c in range(RS_CHUNKS):
@@ -574,7 +578,9 @@
     def _():
         finish(2)
 
-    finish(1)
+    @pl.when(jnp.logical_not(is_first & is_middle))
+    def _():
+        finish(1)
 
     loss_copies = [
         remote(
@@ -594,25 +600,27 @@
 
     @pl.when(is_middle)
     def _():
-        before = jnp.where(is_first, far, next_near)
-        after = jnp.where(is_first, next_near, far)
-
         def pass_all(k, carry):
-            pass_on(jnp.where(k < RS_CHUNKS, before, after), k % RS_CHUNKS)
-            for c in range(RELAY_CHUNKS):
-
-                @pl.when(relays_up & (k == RS_CHUNKS))
-                def _():
-                    pass_sums(c)
+            pass_on(jnp.where(k < RS_CHUNKS, next_near, far), k % RS_CHUNKS)
+
+            @pl.when(is_first & (k == RS_CHUNKS - 1))
+            def _():
+                finish(1)
+
+            @pl.when((in_column[7] | in_column[15]) & (k == 1))
+            def _():
+                pass_flow(2, 0)
+                pass_flow(2, 1)
+
+            @pl.when(in_column[23] & (k == RS_CHUNKS + RS_CHUNKS // 2))
+            def _():
+                pass_flow(3, 0)
 
             return carry
 
         lax.fori_loop(0, 2 * RS_CHUNKS, pass_all, 0)
 
-    @pl.when(relayed_up)
-    def _():
-        for c in range(RELAY_CHUNKS):
-            pass_sums(c)
+    pass_flow(3, 1)
 
     sum_copy(0).wait_recv()
     text_sums = sums[0:rows, :] + sums_in[0].astype(F32)
@@ -688,10 +696,10 @@
         next_down.wait_send()
         back_down.wait_send()
 
-    for c in range(RELAY_CHUNKS):
-        each(captions_first(c) + sums_first(c), (relayed_up, relayed_down) * 2, sent)
-        each(captions_on(c), (relayed_down, is_middle & (passes[c] == 1)), sent)
-        each(sums_on(c)[c == 0 :], (relays_up, relayed_up)[c == 0 :], sent)
+    for kind, c in flow_parts:
+        first, second, sends, passes = flow(kind, c)
+        pl.when(sends)(first.wait_send)
+        pl.when(passes)(second.wait_send)
 
     for copy in core_copies + lab_copies + loss_copies + [sum_copy(i) for i in range(3)]:
         copy.wait_send()
@@ -729,7 +737,7 @@
             pltpu.VMEM((3, rows, width), BF16),
             pltpu.VMEM((2, rows, width), BF16),
             pltpu.VMEM((2, rows, width), BF16),
-            pltpu.VMEM((2, rows, width), BF16),
+            pltpu.VMEM((4, rows, width), BF16),
             dma((3,)),
             dma((2, AG_CHUNKS)),
             dma((CHIPS, AG_CHUNKS)),
@@ -750,10 +758,10 @@
             dma((3,)),
             dma((2,)),
             dma((2,)),
-            dma((2, RELAY_CHUNKS)),
-            dma((2, RELAY_CHUNKS)),
-            dma((2, RELAY_CHUNKS)),
-            pltpu.SemaphoreType.REGULAR((4,)),
+            dma((4, 3)),
+            dma((4, 3)),
+            dma((4, 3)),
+            pltpu.SemaphoreType.REGULAR((5,)),
         ],
         compiler_params=pltpu.CompilerParams(
             collective_id=0, has_side_effects=True, vmem_limit_bytes=48 * 1024 * 1024

time: 65.8 us -> 65.2 us (level); the launches traced: 64.6 us -> 64.7 us
  no operation moved by 1% of the time
where the time goes in v6:
time: 65.2 us; the launch traced here: 64.7 us
  Pallas kernels  58.1 us (89%)
  local copies, waits for them, and re-layouts  4.71 us (7%)
  between operations  1.94 us (3%)
    pallas_call x1, Pallas kernels, per_device(): pl.pallas_call(functools.partial(kernel, blocks), out_shape=[jax.ShapeDty...  58.1 us
    unnamed x9, local copies, waits for them, and re-layouts  4.71 us

profile of v6, /device:TPU:1, one launch (start us, length us, event | category | flops | bytes accessed | tf_op | source)
XLA Modules:
  0.0 64.7 jit_solution(11510558086438538862)
XLA Ops:
  1.9 0.0 copy-start.2
  1.9 0.6 copy-done.2
  2.6 0.0 copy-start
  2.6 1.0 %copy-done = bf16[128,1152]{1,0:T(8,128)(2,1)S(1)} copy-done((bf16[128,1152]{1,0:T(8,128)(2,1)S(1)}, bf16[128,1152]{1,0:T(8,128)(2,1)}, u32[]{:S(2)}) %copy-start) | copy-done | bytes 294936
  3.5 0.0 copy-start.1
  3.5 1.0 %copy-done.1 = bf16[128,1152]{1,0:T(8,128)(2,1)S(1)} copy-done((bf16[128,1152]{1,0:T(8,128)(2,1)S(1)}, bf16[128,1152]{1,0:T(8,128)(2,1)}, u32[]{:S(2)}) %copy-start.1) | copy-done | bytes 294936
  4.5 58.1 %shard_map.76 = (f32[1,128]{1,0:T(1,128)S(1)}, f32[128,1152]{1,0:T(8,128)S(1)}, f32[128,1152]{1,0:T(8,128)S(1)}) custom-call(bf16[128,1152]{1,0:T(8,128)(2,1)S(1)} %copy-done, bf16[128,1152]{1,0:T(8,128)(2,1)S(1)} %copy-done.1, s32[1,128]{1,0:T(1,128)S(1)} %bitcast.2, f32[1]{0:T(128)S(6)} %copy.11.scale_ref, f32[1]{0:T(128)S(6)} %copy.12.bias_ref), custom_call_target="tpu_custom_call" | custom-call | tf_op jit(solution)/shard_map/pallas_call | solution.py:714
  62.6 0.5 copy.13
  63.1 0.8 %copy.14 = f32[128,1152]{1,0:T(8,128)} copy(f32[128,1152]{1,0:T(8,128)S(1)} %get-tuple-element.13) | data formatting | bytes 1179648
  63.9 0.8 %copy.15 = f32[128,1152]{1,0:T(8,128)} copy(f32[128,1152]{1,0:T(8,128)S(1)} %get-tuple-element.14) | data formatting | bytes 1179648
Async XLA Ops:
  1.9 0.7 %copy-start.2 = (s32[128]{0:T(128)S(1)}, s32[128]{0:T(128)}, u32[]{:S(2)}) copy-start(s32[128]{0:T(128)} %param.7) | copy-start | bytes 1540
  2.6 1.0 %copy-start = (bf16[128,1152]{1,0:T(8,128)(2,1)S(1)}, bf16[128,1152]{1,0:T(8,128)(2,1)}, u32[]{:S(2)}) copy-start(bf16[128,1152]{1,0:T(8,128)(2,1)} %images_hbm.1) | copy-start | bytes 884740
  3.5 1.0 %copy-start.1 = (bf16[128,1152]{1,0:T(8,128)(2,1)S(1)}, bf16[128,1152]{1,0:T(8,128)(2,1)}, u32[]{:S(2)}) copy-start(bf16[128,1152]{1,0:T(8,128)(2,1)} %captions_hbm.1) | copy-start | bytes 884740

commit v7 on v6

--- a/solution.py
+++ b/solution.py
@@ -12,10 +12,10 @@
 LINE = 8
 CAPTIONS_VIA = ((24, 0, 48), (8, 48, 48), (16, 96, 32))
 CAPTIONS_UP_VIA = (8, 16)
-SUMS_UP_VIA = (24, 16)
+SUMS_UP_VIA = ((24, 0, 48), (16, 48, 48), (8, 96, 32))
 SUMS_DOWN_VIA = (23, 31)
 AG_CHUNKS = 2
-RS_CHUNKS = 8
+RS_CHUNKS = 4
 MESH = pl.DeviceIdType.MESH
 F32 = jnp.float32
 BF16 = jnp.bfloat16
@@ -180,7 +180,7 @@
         greet(inner_dev(SUMS_DOWN_VIA[0]))
         for offset, _, _ in CAPTIONS_VIA:
             greet(inner_dev(offset))
-        for offset in SUMS_UP_VIA:
+        for offset, _, _ in SUMS_UP_VIA:
             greet(inner_dev(-offset - 1, True))
 
     for offset in CAPTIONS_UP_VIA:
@@ -194,7 +194,7 @@
     def _():
         greet(across_dev)
         greet(inner_dev(SUMS_DOWN_VIA[0] + 1 - blocks, True))
-        for offset in SUMS_UP_VIA:
+        for offset, _, _ in SUMS_UP_VIA:
             greet(inner_dev(-offset))
 
     for offset, _, _ in CAPTIONS_VIA:
@@ -204,7 +204,7 @@
             greet(inner_dev(-offset))
             greet(inner_dev(-offset - 1, True))
 
-    for offset in SUMS_UP_VIA:
+    for offset, _, _ in SUMS_UP_VIA:
 
         @pl.when(in_column[half - 1 - offset])
         def _():
@@ -224,8 +224,8 @@
 
     inner = (y * (3 - y)) // 2
     peers = 4 + jnp.where(is_first, 0, 1) + jnp.where(is_last, 1, 0)
-    inner_peers = 10 * up_edge + 5 * down_edge
-    for offset, count in ((24, 1), (8, 2), (16, 2), (7, 2), (15, 2), (23, 2)):
+    inner_peers = 11 * up_edge + 5 * down_edge
+    for offset, count in ((24, 1), (8, 2), (16, 2), (7, 2), (15, 2), (23, 4)):
         inner_peers = inner_peers + jnp.where(column == offset, count, 0)
     peers = peers + inner * inner_peers
     pl.semaphore_wait(barrier, peers)
@@ -276,8 +276,8 @@
             source, near_dev, far_dev = slot(0), inner_dev(offset), inner_dev(-offset - 1, True)
             target, base, sem, sends, passes = texts, 4 * rows, next_recv.at[1], relayed_down, in_column[offset]
         elif kind == 2:
-            offset = SUMS_UP_VIA[c]
-            begin, size, source = c * 64, 64, back_out.at[1]
+            offset, begin, size = SUMS_UP_VIA[c]
+            source = back_out.at[1]
             near_dev, far_dev = inner_dev(-offset), inner_dev(offset + 1, True)
             target, base, sem = back_in.at[0], 0, back_recv.at[0]
             sends, passes = relayed_up, in_column[half - 1 - offset]
@@ -296,7 +296,7 @@
         )
         return first, second, sends, passes
 
-    flow_parts = [(0, 0), (0, 1), (1, 0), (1, 1), (1, 2), (2, 0), (2, 1), (3, 0), (3, 1)]
+    flow_parts = [(0, 0), (0, 1), (1, 0), (1, 1), (1, 2), (2, 0), (2, 1), (2, 2), (3, 0), (3, 1)]
 
     def send_flow(kind, c):
         first, _, sends, _ = flow(kind, c)
@@ -429,7 +429,7 @@
                 pl.semaphore_wait(ready.at[3], 1)
                 pl.semaphore_wait(ready.at[4], 1)
 
-        for c in range(2):
+        for c in range(1 + i):
             send_flow(4 - i, c)
 
     back_down = remote(back_out.at[0], back_in.at[1], back_send.at[0], back_recv.at[1], down_dev)
@@ -535,7 +535,7 @@
             for c in range(AG_CHUNKS):
                 take(far, c)
 
-        @pl.when((u == 6) & (in_column[8] | in_column[16]))
+        @pl.when((u == 5) & (in_column[8] | in_column[16]))
         def _():
             pass_flow(0, 0)
             pass_flow(0, 1)
@@ -607,10 +607,10 @@
             def _():
                 finish(1)
 
-            @pl.when((in_column[7] | in_column[15]) & (k == 1))
+            @pl.when((in_column[7] | in_column[15] | in_column[23]) & (k == 1))
             def _():
-                pass_flow(2, 0)
-                pass_flow(2, 1)
+                for c in range(3):
+                    pass_flow(2, c)
 
             @pl.when(in_column[23] & (k == RS_CHUNKS + RS_CHUNKS // 2))
             def _():
@@ -629,7 +629,7 @@
     back_up.wait_recv()
     text_sums = text_sums + back_in[0].astype(F32)
     text_float, text_length = unit_rows(captions[...])
-    text_out[...] = through_norm(text_sums, text_float, text_length)
+    text_out[...] = through_norm(text_sums, text_float, text_length).astype(BF16)
 
     loss_total = loss_part[y]
     for d in (1, 2, 3):
@@ -655,7 +655,7 @@
         parts[y] += end_in[y].astype(F32)
 
     image_float, image_length = unit_rows(images[...])
-    image_out[...] = through_norm(parts[y], image_float, image_length)
+    image_out[...] = through_norm(parts[y], image_float, image_length).astype(BF16)
 
     for c in range(AG_CHUNKS):
 
@@ -715,8 +715,8 @@
         functools.partial(kernel, blocks),
         out_shape=[
             jax.ShapeDtypeStruct((1, rows), F32),
-            jax.ShapeDtypeStruct((rows, width), F32),
-            jax.ShapeDtypeStruct((rows, width), F32),
+            jax.ShapeDtypeStruct((rows, width), BF16),
+            jax.ShapeDtypeStruct((rows, width), BF16),
         ],
         in_specs=[hbm, hbm, hbm, smem, smem],
         out_specs=[vmem, vmem, vmem],
@@ -764,10 +764,10 @@
             pltpu.SemaphoreType.REGULAR((5,)),
         ],
         compiler_params=pltpu.CompilerParams(
-            collective_id=0, has_side_effects=True, vmem_limit_bytes=48 * 1024 * 1024
+            collective_id=0, has_side_effects=True, vmem_limit_bytes=60 * 1024 * 1024
         ),
     )(images, captions, labels.reshape(1, rows), logit_scale, logit_bias)
-    return (loss.reshape(rows), image_grad, text_grad)
+    return (loss.reshape(rows), image_grad.astype(F32), text_grad.astype(F32))
 
 
 def solution(mesh):

time: 65.2 us -> 64 us (0.982)
  local copies, waits for them, and re-layouts: 4.71 us -> 0.52 us
  other arithmetic: 0 us -> 2.71 us
    unnamed x9 -> x5, local copies, waits for them, and re-layouts: 4.71 us -> 0.52 us
    convert_element_type x0 -> x2, other arithmetic: none -> 2.71 us  [per_device(): return (loss.reshape(rows), image_grad.astype(F32), text_grad.astype(F32))]
where the time goes in v7:
time: 64 us; the launch traced here: 63.4 us
  Pallas kernels  58.2 us (91%)
  other arithmetic  2.71 us (4%)
  between operations  1.94 us (3%)
    pallas_call x1, Pallas kernels, per_device(): pl.pallas_call(functools.partial(kernel, blocks), out_shape=[jax.ShapeDty...  58.2 us
    convert_element_type x2, other arithmetic, per_device(): return (loss.reshape(rows), image_grad.astype(F32), text_grad.astype(F32))  2.71 us

profile of v7, /device:TPU:1, one launch (start us, length us, event | category | flops | bytes accessed | tf_op | source)
XLA Modules:
  0.0 63.4 jit_solution(9868299145852802496)
XLA Ops:
  1.9 58.2 %shard_map.76 = (f32[1,128]{1,0:T(1,128)}, bf16[128,1152]{1,0:T(8,128)(2,1)}, bf16[128,1152]{1,0:T(8,128)(2,1)}) custom-call(bf16[128,1152]{1,0:T(8,128)(2,1)} %images_hbm.1, bf16[128,1152]{1,0:T(8,128)(2,1)} %captions_hbm.1, s32[1,128]{1,0:T(1,128)} %bitcast.2, f32[1]{0:T(128)S(6)} %copy.9.scale_ref, f32[1]{0:T(128)S(6)} %copy.10.bias_ref), custom_call_target="tpu_custom_call" | custom-call | tf_op jit(solution)/shard_map/pallas_call | solution.py:714
  60.1 0.0 copy-start
  60.2 1.9 %convert_element_type.6 = f32[128,1152]{1,0:T(8,128)} convert(bf16[128,1152]{1,0:T(8,128)(2,1)} %get-tuple-element.7) | non-fusion elementwise | flops 147456 | bytes 884736 | tf_op jit(solution)/shard_map/convert_element_type | solution.py:770
  62.0 0.0 copy-done
  62.0 0.0 copy-start.1
  62.0 0.9 %convert_element_type.7 = f32[128,1152]{1,0:T(8,128)} convert(bf16[128,1152]{1,0:T(8,128)(2,1)S(1)} %copy-done) | non-fusion elementwise | flops 147456 | bytes 884736 | tf_op jit(solution)/shard_map/convert_element_type | solution.py:770
  62.9 0.0 copy-done.1
  62.9 0.5 copy.11
Async XLA Ops:
  60.1 1.9 %copy-start = (bf16[128,1152]{1,0:T(8,128)(2,1)S(1)}, bf16[128,1152]{1,0:T(8,128)(2,1)}, u32[]{:S(2)}) copy-start(bf16[128,1152]{1,0:T(8,128)(2,1)} %get-tuple-element.8) | copy-start | bytes 884740
  62.0 0.9 %copy-start.1 = (f32[1,128]{1,0:T(1,128)S(1)}, f32[1,128]{1,0:T(1,128)}, u32[]{:S(2)}) copy-start(f32[1,128]{1,0:T(1,128)} %get-tuple-element.6) | copy-start | bytes 1540

commit v8 on v7

--- a/solution.py
+++ b/solution.py
@@ -449,7 +449,7 @@
     usual_order = [y, near, near, near, y, y, next_near, next_near, next_near, far, far, far]
     late_order = [y, near, near, y, next_near, next_near, near, y, next_near, far, far, far]
     first_end_order = [y, near, near, y, next_near, next_near, next_near, far, far, far, near, y]
-    first_order = [y, near, near, y, next_near, next_near, far, far, far, next_near, near, y]
+    first_order = [y, near, near, y, next_near, next_near, far, far, next_near, far, near, y]
 
     def step(u, carry):
         s = chosen(u, usual_order, first_order, first_end_order, late_order)
@@ -520,6 +520,11 @@
         def _():
             core_copies[2].wait_recv()
 
+        @pl.when((u == 4) & (in_column[8] | in_column[16]))
+        def _():
+            pass_flow(0, 0)
+            pass_flow(0, 1)
+
         @pl.when((u == 4) & is_middle)
         def _():
             for c in range(1, AG_CHUNKS):
@@ -534,11 +539,6 @@
         def _():
             for c in range(AG_CHUNKS):
                 take(far, c)
-
-        @pl.when((u == 5) & (in_column[8] | in_column[16]))
-        def _():
-            pass_flow(0, 0)
-            pass_flow(0, 1)
 
         @pl.when((u == jnp.where(is_end, 6, 8)) & is_first)
         def _():
@@ -546,7 +546,7 @@
             core_copies[1].start()
             core_copies[1].wait_recv()
 
-        @pl.when((u == jnp.where(is_end, 11, 9)) & is_first)
+        @pl.when(((u == jnp.where(is_end, 11, 9)) & is_first) | ((u == 11) & relayed_up))
         def _():
             finish(2)
 
@@ -574,7 +574,7 @@
 
     lax.fori_loop(0, 3 * CHIPS, step, 0)
 
-    @pl.when(not_first)
+    @pl.when(not_first & jnp.logical_not(relayed_up))
     def _():
         finish(2)
 
@@ -600,6 +600,9 @@
 
     @pl.when(is_middle)
     def _():
+        for c in range(3):
+            pass_flow(2, c)
+
         def pass_all(k, carry):
             pass_on(jnp.where(k < RS_CHUNKS, next_near, far), k % RS_CHUNKS)
 
@@ -607,11 +610,6 @@
             def _():
                 finish(1)
 
-            @pl.when((in_column[7] | in_column[15] | in_column[23]) & (k == 1))
-            def _():
-                for c in range(3):
-                    pass_flow(2, c)
-
             @pl.when(in_column[23] & (k == RS_CHUNKS + RS_CHUNKS // 2))
             def _():
                 pass_flow(3, 0)
@@ -621,15 +619,6 @@
         lax.fori_loop(0, 2 * RS_CHUNKS, pass_all, 0)
 
     pass_flow(3, 1)
-
-    sum_copy(0).wait_recv()
-    text_sums = sums[0:rows, :] + sums_in[0].astype(F32)
-    back_down.wait_recv()
-    text_sums = text_sums + back_in[1].astype(F32)
-    back_up.wait_recv()
-    text_sums = text_sums + back_in[0].astype(F32)
-    text_float, text_length = unit_rows(captions[...])
-    text_out[...] = through_norm(text_sums, text_float, text_length).astype(BF16)
 
     loss_total = loss_part[y]
     for d in (1, 2, 3):
@@ -656,6 +645,15 @@
 
     image_float, image_length = unit_rows(images[...])
     image_out[...] = through_norm(parts[y], image_float, image_length).astype(BF16)
+
+    sum_copy(0).wait_recv()
+    text_sums = sums[0:rows, :] + sums_in[0].astype(F32)
+    back_down.wait_recv()
+    text_sums = text_sums + back_in[1].astype(F32)
+    text_float, text_length = unit_rows(captions[...])
+    back_up.wait_recv()
+    text_sums = text_sums + back_in[0].astype(F32)
+    text_out[...] = through_norm(text_sums, text_float, text_length).astype(BF16)
 
     for c in range(AG_CHUNKS):
 

time: 64 us -> 63.4 us (level)
  the two profiles are of different devices: /device:TPU:1 before, /device:TPU:8 now
where the time goes in v8:
time: 63.4 us; the launch traced here: 63.3 us
  Pallas kernels  58.1 us (92%)
  other arithmetic  2.71 us (4%)
  between operations  1.94 us (3%)
    pallas_call x1, Pallas kernels, per_device(): pl.pallas_call(functools.partial(kernel, blocks), out_shape=[jax.ShapeDty...  58.1 us
    convert_element_type x2, other arithmetic, per_device(): return (loss.reshape(rows), image_grad.astype(F32), text_grad.astype(F32))  2.71 us

profile of v8, /device:TPU:8, one launch (start us, length us, event | category | flops | bytes accessed | tf_op | source)
XLA Modules:
  0.0 63.3 jit_solution(7992903417371093934)
XLA Ops:
  1.9 58.1 %shard_map.76 = (f32[1,128]{1,0:T(1,128)}, bf16[128,1152]{1,0:T(8,128)(2,1)}, bf16[128,1152]{1,0:T(8,128)(2,1)}) custom-call(bf16[128,1152]{1,0:T(8,128)(2,1)} %images_hbm.1, bf16[128,1152]{1,0:T(8,128)(2,1)} %captions_hbm.1, s32[1,128]{1,0:T(1,128)} %bitcast.2, f32[1]{0:T(128)S(6)} %copy.9.scale_ref, f32[1]{0:T(128)S(6)} %copy.10.bias_ref), custom_call_target="tpu_custom_call" | custom-call | tf_op jit(solution)/shard_map/pallas_call | solution.py:712
  60.0 0.0 copy-start
  60.0 1.9 %convert_element_type.6 = f32[128,1152]{1,0:T(8,128)} convert(bf16[128,1152]{1,0:T(8,128)(2,1)} %get-tuple-element.7) | non-fusion elementwise | flops 147456 | bytes 884736 | tf_op jit(solution)/shard_map/convert_element_type | solution.py:768
  61.9 0.0 copy-done
  61.9 0.0 copy-start.1
  61.9 0.9 %convert_element_type.7 = f32[128,1152]{1,0:T(8,128)} convert(bf16[128,1152]{1,0:T(8,128)(2,1)S(1)} %copy-done) | non-fusion elementwise | flops 147456 | bytes 884736 | tf_op jit(solution)/shard_map/convert_element_type | solution.py:768
  62.7 0.0 copy-done.1
  62.7 0.5 copy.11
Async XLA Ops:
  60.0 1.9 %copy-start = (bf16[128,1152]{1,0:T(8,128)(2,1)S(1)}, bf16[128,1152]{1,0:T(8,128)(2,1)}, u32[]{:S(2)}) copy-start(bf16[128,1152]{1,0:T(8,128)(2,1)} %get-tuple-element.8) | copy-start | bytes 884740
  61.9 0.9 %copy-start.1 = (f32[1,128]{1,0:T(1,128)S(1)}, f32[1,128]{1,0:T(1,128)}, u32[]{:S(2)}) copy-start(f32[1,128]{1,0:T(1,128)} %get-tuple-element.6) | copy-start | bytes 1540

commit v9 on v8

--- a/solution.py
+++ b/solution.py
@@ -12,7 +12,7 @@
 LINE = 8
 CAPTIONS_VIA = ((24, 0, 48), (8, 48, 48), (16, 96, 32))
 CAPTIONS_UP_VIA = (8, 16)
-SUMS_UP_VIA = ((24, 0, 48), (16, 48, 48), (8, 96, 32))
+SUMS_UP_VIA = ((24, 0, 64), (16, 64, 32), (8, 96, 32))
 SUMS_DOWN_VIA = (23, 31)
 AG_CHUNKS = 2
 RS_CHUNKS = 4

time: 63.4 us -> 61.5 us (0.970)
  the two profiles are of different devices: /device:TPU:8 before, /device:TPU:1 now
where the time goes in v9:
time: 61.5 us; the launch traced here: 61.1 us
  Pallas kernels  56 us (91%)
  other arithmetic  2.71 us (4%)
  between operations  1.94 us (3%)
    pallas_call x1, Pallas kernels, per_device(): pl.pallas_call(functools.partial(kernel, blocks), out_shape=[jax.ShapeDty...  56 us
    convert_element_type x2, other arithmetic, per_device(): return (loss.reshape(rows), image_grad.astype(F32), text_grad.astype(F32))  2.71 us

profile of v9, /device:TPU:1, one launch (start us, length us, event | category | flops | bytes accessed | tf_op | source)
XLA Modules:
  0.0 61.1 jit_solution(5803463332271081135)
XLA Ops:
  1.9 56.0 %shard_map.76 = (f32[1,128]{1,0:T(1,128)}, bf16[128,1152]{1,0:T(8,128)(2,1)}, bf16[128,1152]{1,0:T(8,128)(2,1)}) custom-call(bf16[128,1152]{1,0:T(8,128)(2,1)} %images_hbm.1, bf16[128,1152]{1,0:T(8,128)(2,1)} %captions_hbm.1, s32[1,128]{1,0:T(1,128)} %bitcast.2, f32[1]{0:T(128)S(6)} %copy.9.scale_ref, f32[1]{0:T(128)S(6)} %copy.10.bias_ref), custom_call_target="tpu_custom_call" | custom-call | tf_op jit(solution)/shard_map/pallas_call | solution.py:712
  57.9 0.0 copy-start
  57.9 1.9 %convert_element_type.6 = f32[128,1152]{1,0:T(8,128)} convert(bf16[128,1152]{1,0:T(8,128)(2,1)} %get-tuple-element.7) | non-fusion elementwise | flops 147456 | bytes 884736 | tf_op jit(solution)/shard_map/convert_element_type | solution.py:768
  59.8 0.0 copy-done
  59.8 0.0 copy-start.1
  59.8 0.9 %convert_element_type.7 = f32[128,1152]{1,0:T(8,128)} convert(bf16[128,1152]{1,0:T(8,128)(2,1)S(1)} %copy-done) | non-fusion elementwise | flops 147456 | bytes 884736 | tf_op jit(solution)/shard_map/convert_element_type | solution.py:768
  60.6 0.0 copy-done.1
  60.6 0.5 copy.11
Async XLA Ops:
  57.9 1.9 %copy-start = (bf16[128,1152]{1,0:T(8,128)(2,1)S(1)}, bf16[128,1152]{1,0:T(8,128)(2,1)}, u32[]{:S(2)}) copy-start(bf16[128,1152]{1,0:T(8,128)(2,1)} %get-tuple-element.8) | copy-start | bytes 884740
  59.8 0.9 %copy-start.1 = (f32[1,128]{1,0:T(1,128)S(1)}, f32[1,128]{1,0:T(1,128)}, u32[]{:S(2)}) copy-start(f32[1,128]{1,0:T(1,128)} %get-tuple-element.6) | copy-start | bytes 1540

commit v10 on v9

--- a/solution.py
+++ b/solution.py
@@ -12,7 +12,7 @@
 LINE = 8
 CAPTIONS_VIA = ((24, 0, 48), (8, 48, 48), (16, 96, 32))
 CAPTIONS_UP_VIA = (8, 16)
-SUMS_UP_VIA = ((24, 0, 64), (16, 64, 32), (8, 96, 32))
+SUMS_UP_VIA = ((24, 0, 80), (16, 80, 32), (8, 112, 16))
 SUMS_DOWN_VIA = (23, 31)
 AG_CHUNKS = 2
 RS_CHUNKS = 4

time: 61.5 us -> 61.3 us (level)
  no operation moved by 1% of the time
where the time goes in v10:
time: 61.3 us; the launch traced here: 61.1 us
  Pallas kernels  56 us (91%)
  other arithmetic  2.71 us (4%)
  between operations  1.94 us (3%)
    pallas_call x1, Pallas kernels, per_device(): pl.pallas_call(functools.partial(kernel, blocks), out_shape=[jax.ShapeDty...  56 us
    convert_element_type x2, other arithmetic, per_device(): return (loss.reshape(rows), image_grad.astype(F32), text_grad.astype(F32))  2.71 us

profile of v10, /device:TPU:1, one launch (start us, length us, event | category | flops | bytes accessed | tf_op | source)
XLA Modules:
  0.0 61.1 jit_solution(7614248660517264901)
XLA Ops:
  1.9 56.0 %shard_map.76 = (f32[1,128]{1,0:T(1,128)}, bf16[128,1152]{1,0:T(8,128)(2,1)}, bf16[128,1152]{1,0:T(8,128)(2,1)}) custom-call(bf16[128,1152]{1,0:T(8,128)(2,1)} %images_hbm.1, bf16[128,1152]{1,0:T(8,128)(2,1)} %captions_hbm.1, s32[1,128]{1,0:T(1,128)} %bitcast.2, f32[1]{0:T(128)S(6)} %copy.9.scale_ref, f32[1]{0:T(128)S(6)} %copy.10.bias_ref), custom_call_target="tpu_custom_call" | custom-call | tf_op jit(solution)/shard_map/pallas_call | solution.py:712
  57.9 0.0 copy-start
  57.9 1.9 %convert_element_type.6 = f32[128,1152]{1,0:T(8,128)} convert(bf16[128,1152]{1,0:T(8,128)(2,1)} %get-tuple-element.7) | non-fusion elementwise | flops 147456 | bytes 884736 | tf_op jit(solution)/shard_map/convert_element_type | solution.py:768
  59.8 0.0 copy-done
  59.8 0.0 copy-start.1
  59.8 0.9 %convert_element_type.7 = f32[128,1152]{1,0:T(8,128)} convert(bf16[128,1152]{1,0:T(8,128)(2,1)S(1)} %copy-done) | non-fusion elementwise | flops 147456 | bytes 884736 | tf_op jit(solution)/shard_map/convert_element_type | solution.py:768
  60.6 0.0 copy-done.1
  60.6 0.5 copy.11
Async XLA Ops:
  57.9 1.9 %copy-start = (bf16[128,1152]{1,0:T(8,128)(2,1)S(1)}, bf16[128,1152]{1,0:T(8,128)(2,1)}, u32[]{:S(2)}) copy-start(bf16[128,1152]{1,0:T(8,128)(2,1)} %get-tuple-element.8) | copy-start | bytes 884740
  59.8 0.9 %copy-start.1 = (f32[1,128]{1,0:T(1,128)S(1)}, f32[1,128]{1,0:T(1,128)}, u32[]{:S(2)}) copy-start(f32[1,128]{1,0:T(1,128)} %get-tuple-element.6) | copy-start | bytes 1540
